TPU v7x, 128 devices: a whole 4x4x4 slice. The times are simulated.
128 devices in a mesh: dp: 4 (over z), ctx: 8 (over y_lo, x), tensor: 4 (over y_hi, core).
Axes of the slice: x: 4, y: 4 (y_hi: 2, y_lo: 2; y = y_hi * 2 + y_lo), z: 4, core: 2. Of those that a mesh axis runs over, the one named last changes fastest.
Arguments:
- inputs: bfloat16 [4, 2048, 2048], P('dp', 'ctx'), may hold values from -6 to 6
- segments: int32 [4, 2048], P('dp', 'ctx'), may hold values from 0 to 8, as said below
- w_query: bfloat16 [2048, 2048], P(None, 'tensor'), may hold values from -0.125 to 0.125
- w_key: bfloat16 [2048, 2048], P(None, 'tensor'), may hold values from -0.125 to 0.125
- w_value: bfloat16 [2048, 2048], P(None, 'tensor'), may hold values from -0.125 to 0.125
- w_out: bfloat16 [2048, 2048], P('tensor'), may hold values from -0.125 to 0.125
- q_gain: float32 [16, 128], P('tensor'), may hold values from 0.25 to 1.75
- k_gain: float32 [16, 128], P('tensor'), may hold values from 0.25 to 1.75
- attn_gain: float32 [2048], replicated, may hold values from 0.25 to 1.75
- w_gate: bfloat16 [2048, 8192], P(None, 'tensor'), may hold values from -0.125 to 0.125
- w_up: bfloat16 [2048, 8192], P(None, 'tensor'), may hold values from -0.125 to 0.125
- w_down: bfloat16 [8192, 2048], P('tensor'), may hold values from -0.0625 to 0.0625
- mlp_gain: float32 [2048], replicated, may hold values from 0.25 to 1.75
- cotangent: bfloat16 [4, 2048, 2048], P('dp', 'ctx'), may hold values from -6 to 6
Outputs:
- outputs: bfloat16 [4, 2048, 2048], P('dp', 'ctx')
- input_grad: bfloat16 [4, 2048, 2048], P('dp', 'ctx')
- grad_query: float32 [2048, 2048], P(('dp', 'ctx'), 'tensor')
- grad_key: float32 [2048, 2048], P(('dp', 'ctx'), 'tensor')
- grad_value: float32 [2048, 2048], P(('dp', 'ctx'), 'tensor')
- grad_out: float32 [2048, 2048], P('tensor', ('dp', 'ctx'))
- grad_q_gain: float32 [16, 128], P('tensor', ('dp', 'ctx'))
- grad_k_gain: float32 [16, 128], P('tensor', ('dp', 'ctx'))
- grad_attn_gain: float32 [2048], P(('dp', 'ctx'))
- grad_gate: float32 [2048, 8192], P(('dp', 'ctx'), 'tensor')
- grad_up: float32 [2048, 8192], P(('dp', 'ctx'), 'tensor')
- grad_down: float32 [8192, 2048], P('tensor', ('dp', 'ctx'))
- grad_mlp_gain: float32 [2048], P(('dp', 'ctx'))
Inputs may be any that keep to these rules, and one draw needn't show every extreme that they name: `segments`: never falling along a sequence; 0 at each sequence's first token and 8 at its last.
All inputs are finite; a program needn't handle non-finite values.
Results may differ from a plain program's by a relative error of at most 0.035.
Values may be sent and summed in bfloat16 or wider, within the bound.
A program may use at most 192 MiB of HBM per device.

v0:
```python
import jax
import jax.numpy as jnp
from jax import lax
from jax.sharding import PartitionSpec as P

epsilon = 1e-06


def norm_backward(values_in, scale_col, gain_row, grad_in, column_sum, width):
    return scale_col * gain_row * grad_in - values_in * scale_col**3 * column_sum / width


def masked_scores(query_heads, key_heads, counted, scale):
    scores = (
        jnp.einsum("qhd,khd->hqk", query_heads, key_heads, preferred_element_type=jnp.float32)
        * scale
    )
    return jnp.where(counted[None], scores, -1e30)


def per_device(
    inputs,
    segments,
    w_query,
    w_key,
    w_value,
    w_out,
    q_gain,
    k_gain,
    attn_gain,
    w_gate,
    w_up,
    w_down,
    mlp_gain,
    cotangent,
):
    features = inputs[0]
    seg_local = segments[0]
    shard_len = features.shape[0]
    width = features.shape[1]
    local_heads = q_gain.shape[0]
    head_dim = q_gain.shape[1]
    scale = head_dim ** (-0.5)
    q_gain_row = q_gain.reshape(1, -1)
    k_gain_row = k_gain.reshape(1, -1)
    q_raw = jnp.dot(features, w_query, preferred_element_type=jnp.float32)
    k_raw = jnp.dot(features, w_key, preferred_element_type=jnp.float32)
    value_low = jnp.dot(features, w_value, preferred_element_type=jnp.float32).astype(jnp.bfloat16)
    q_square, k_square = lax.psum(
        (jnp.sum(q_raw * q_raw, axis=1), jnp.sum(k_raw * k_raw, axis=1)), "tensor"
    )
    q_scale = lax.rsqrt(q_square[:, None] / width + epsilon)
    k_scale = lax.rsqrt(k_square[:, None] / width + epsilon)
    query_low = (q_raw * q_scale * q_gain_row).astype(jnp.bfloat16)
    key_low = (k_raw * k_scale * k_gain_row).astype(jnp.bfloat16)
    seg_low = seg_local.astype(jnp.bfloat16)
    keys_all, values_all, seg_all = (
        lax.all_gather(key_low, "ctx", axis=0, tiled=True),
        lax.all_gather(value_low, "ctx", axis=0, tiled=True),
        lax.all_gather(seg_low, "ctx", axis=0, tiled=True),
    )
    total_len = keys_all.shape[0]
    query_place = lax.axis_index("ctx") * shard_len + jnp.arange(shard_len, dtype=jnp.int32)
    key_place = jnp.arange(total_len, dtype=jnp.int32)
    query_heads = query_low.reshape(shard_len, local_heads, head_dim)
    counted = (key_place[None, :] <= query_place[:, None]) & (seg_all[None, :] == seg_low[:, None])
    scores = masked_scores(
        query_heads, keys_all.reshape(total_len, local_heads, head_dim), counted, scale
    )
    row_max = jnp.max(scores, axis=2, keepdims=True)
    exps = jnp.exp(scores - row_max)
    row_total = jnp.sum(exps, axis=2, keepdims=True)
    probs_low = (exps / row_total).astype(jnp.bfloat16)
    log_total = row_max + jnp.log(row_total)
    attended = jnp.einsum(
        "hqk,khd->qhd",
        probs_low,
        values_all.reshape(total_len, local_heads, head_dim),
        preferred_element_type=jnp.float32,
    )
    attended_low = attended.reshape(shard_len, local_heads * head_dim).astype(jnp.bfloat16)
    attn_out = lax.psum(jnp.dot(attended_low, w_out, preferred_element_type=jnp.float32), "tensor")
    a_scale = lax.rsqrt(jnp.mean(attn_out * attn_out, axis=1, keepdims=True) + epsilon)
    hidden_state = features.astype(jnp.float32) + attn_out * a_scale * attn_gain
    hidden_low = hidden_state.astype(jnp.bfloat16)
    gate = jnp.dot(hidden_low, w_gate, preferred_element_type=jnp.float32)
    upward = jnp.dot(hidden_low, w_up, preferred_element_type=jnp.float32)
    sigma = jax.nn.sigmoid(gate)
    activated = gate * sigma
    mixed_low = (activated * upward).astype(jnp.bfloat16)
    mlp_out = lax.psum(jnp.dot(mixed_low, w_down, preferred_element_type=jnp.float32), "tensor")
    z_scale = lax.rsqrt(jnp.mean(mlp_out * mlp_out, axis=1, keepdims=True) + epsilon)
    outputs = (hidden_state + mlp_out * z_scale * mlp_gain).astype(jnp.bfloat16)
    grad_top = cotangent[0].astype(jnp.float32)
    grad_mlp_gain = jnp.sum(grad_top * mlp_out * z_scale, axis=0)
    mlp_sum_col = jnp.sum(grad_top * mlp_gain * mlp_out, axis=1, keepdims=True)
    d_mlp_low = norm_backward(mlp_out, z_scale, mlp_gain, grad_top, mlp_sum_col, width).astype(
        jnp.bfloat16
    )
    grad_down = jnp.einsum("tf,td->fd", mixed_low, d_mlp_low, preferred_element_type=jnp.float32)
    d_mixed = jnp.einsum("td,fd->tf", d_mlp_low, w_down, preferred_element_type=jnp.float32)
    d_up = (d_mixed * activated).astype(jnp.bfloat16)
    d_gate = (d_mixed * upward * sigma * (1.0 + gate * (1.0 - sigma))).astype(jnp.bfloat16)
    grad_gate = jnp.einsum("td,tf->df", hidden_low, d_gate, preferred_element_type=jnp.float32)
    grad_up = jnp.einsum("td,tf->df", hidden_low, d_up, preferred_element_type=jnp.float32)
    mlp_back = jnp.einsum(
        "tf,df->td", d_gate, w_gate, preferred_element_type=jnp.float32
    ) + jnp.einsum("tf,df->td", d_up, w_up, preferred_element_type=jnp.float32)
    d_hidden = grad_top + lax.psum(mlp_back, "tensor")
    grad_attn_gain = jnp.sum(d_hidden * attn_out * a_scale, axis=0)
    attn_sum_col = jnp.sum(d_hidden * attn_gain * attn_out, axis=1, keepdims=True)
    d_attn_low = norm_backward(attn_out, a_scale, attn_gain, d_hidden, attn_sum_col, width).astype(
        jnp.bfloat16
    )
    grad_out = jnp.einsum("tc,td->cd", attended_low, d_attn_low, preferred_element_type=jnp.float32)
    d_attended = jnp.einsum(
        "td,cd->tc", d_attn_low, w_out, preferred_element_type=jnp.float32
    ).astype(jnp.bfloat16)
    keys_back, values_back, seg_back = (keys_all, values_all, seg_all)
    key_heads = keys_back.reshape(total_len, local_heads, head_dim)
    value_heads = values_back.reshape(total_len, local_heads, head_dim)
    counted_back = (key_place[None, :] <= query_place[:, None]) & (
        seg_back[None, :] == seg_low[:, None]
    )
    probs = jnp.exp(masked_scores(query_heads, key_heads, counted_back, scale) - log_total)
    probs_back = probs.astype(jnp.bfloat16)
    attended_heads = d_attended.reshape(shard_len, local_heads, head_dim)
    d_probs = jnp.einsum(
        "qhd,khd->hqk", attended_heads, value_heads, preferred_element_type=jnp.float32
    )
    delta = jnp.sum(probs * d_probs, axis=2, keepdims=True)
    d_scores = (probs * (d_probs - delta)).astype(jnp.bfloat16)
    d_queries = scale * jnp.einsum(
        "hqk,khd->qhd", d_scores, key_heads, preferred_element_type=jnp.float32
    )
    d_keys_all = scale * jnp.einsum(
        "hqk,qhd->khd", d_scores, query_heads, preferred_element_type=jnp.float32
    )
    d_values_all = jnp.einsum(
        "hqk,qhd->khd", probs_back, attended_heads, preferred_element_type=jnp.float32
    )
    d_keys, d_values = (
        lax.psum_scatter(
            d_keys_all.reshape(total_len, local_heads * head_dim),
            "ctx",
            scatter_dimension=0,
            tiled=True,
        ),
        lax.psum_scatter(
            d_values_all.reshape(total_len, local_heads * head_dim),
            "ctx",
            scatter_dimension=0,
            tiled=True,
        ),
    )
    d_values_low = d_values.astype(jnp.bfloat16)
    d_queries = d_queries.reshape(shard_len, local_heads * head_dim)
    q_column_sum, k_column_sum = lax.psum(
        (
            jnp.sum(d_queries * q_gain_row * q_raw, axis=1),
            jnp.sum(d_keys * k_gain_row * k_raw, axis=1),
        ),
        "tensor",
    )
    grad_q_gain = jnp.sum(d_queries * q_raw * q_scale, axis=0).reshape(local_heads, head_dim)
    grad_k_gain = jnp.sum(d_keys * k_raw * k_scale, axis=0).reshape(local_heads, head_dim)
    d_q_low = norm_backward(
        q_raw, q_scale, q_gain_row, d_queries, q_column_sum[:, None], width
    ).astype(jnp.bfloat16)
    d_k_low = norm_backward(
        k_raw, k_scale, k_gain_row, d_keys, k_column_sum[:, None], width
    ).astype(jnp.bfloat16)
    grad_query = jnp.einsum("td,tc->dc", features, d_q_low, preferred_element_type=jnp.float32)
    grad_key = jnp.einsum("td,tc->dc", features, d_k_low, preferred_element_type=jnp.float32)
    grad_value = jnp.einsum("td,tc->dc", features, d_values_low, preferred_element_type=jnp.float32)
    attn_back = (
        jnp.einsum("tc,dc->td", d_q_low, w_query, preferred_element_type=jnp.float32)
        + jnp.einsum("tc,dc->td", d_k_low, w_key, preferred_element_type=jnp.float32)
        + jnp.einsum("tc,dc->td", d_values_low, w_value, preferred_element_type=jnp.float32)
    )
    input_grad = (
        d_hidden + lax.psum(attn_back.astype(jnp.bfloat16), "tensor").astype(jnp.float32)
    ).astype(jnp.bfloat16)
    local_grads = (
        grad_query,
        grad_key,
        grad_value,
        grad_out,
        grad_q_gain,
        grad_k_gain,
        grad_attn_gain,
        grad_gate,
        grad_up,
        grad_down,
        grad_mlp_gain,
    )
    summed = (
        lax.psum_scatter(
            local_grads[0].astype(jnp.bfloat16), ("dp", "ctx"), scatter_dimension=0, tiled=True
        ).astype(jnp.float32),
        lax.psum_scatter(
            local_grads[1].astype(jnp.bfloat16), ("dp", "ctx"), scatter_dimension=0, tiled=True
        ).astype(jnp.float32),
        lax.psum_scatter(
            local_grads[2].astype(jnp.bfloat16), ("dp", "ctx"), scatter_dimension=0, tiled=True
        ).astype(jnp.float32),
        lax.psum_scatter(
            local_grads[3].astype(jnp.bfloat16), ("dp", "ctx"), scatter_dimension=1, tiled=True
        ).astype(jnp.float32),
        lax.psum_scatter(
            local_grads[4].astype(jnp.bfloat16), ("dp", "ctx"), scatter_dimension=1, tiled=True
        ).astype(jnp.float32),
        lax.psum_scatter(
            local_grads[5].astype(jnp.bfloat16), ("dp", "ctx"), scatter_dimension=1, tiled=True
        ).astype(jnp.float32),
        lax.psum_scatter(
            local_grads[6].astype(jnp.bfloat16), ("dp", "ctx"), scatter_dimension=0, tiled=True
        ).astype(jnp.float32),
        lax.psum_scatter(
            local_grads[7].astype(jnp.bfloat16), ("dp", "ctx"), scatter_dimension=0, tiled=True
        ).astype(jnp.float32),
        lax.psum_scatter(
            local_grads[8].astype(jnp.bfloat16), ("dp", "ctx"), scatter_dimension=0, tiled=True
        ).astype(jnp.float32),
        lax.psum_scatter(
            local_grads[9].astype(jnp.bfloat16), ("dp", "ctx"), scatter_dimension=1, tiled=True
        ).astype(jnp.float32),
        lax.psum_scatter(
            local_grads[10].astype(jnp.bfloat16), ("dp", "ctx"), scatter_dimension=0, tiled=True
        ).astype(jnp.float32),
    )
    return (outputs[None], input_grad[None]) + tuple(summed)


def solution(mesh):
    in_specs = (
        P("dp", "ctx", None),
        P("dp", "ctx"),
        P(None, "tensor"),
        P(None, "tensor"),
        P(None, "tensor"),
        P("tensor", None),
        P("tensor", None),
        P("tensor", None),
        P(),
        P(None, "tensor"),
        P(None, "tensor"),
        P("tensor", None),
        P(),
        P("dp", "ctx", None),
    )
    out_specs = (
        P("dp", "ctx", None),
        P("dp", "ctx", None),
        P(("dp", "ctx"), "tensor"),
        P(("dp", "ctx"), "tensor"),
        P(("dp", "ctx"), "tensor"),
        P("tensor", ("dp", "ctx")),
        P("tensor", ("dp", "ctx")),
        P("tensor", ("dp", "ctx")),
        P(("dp", "ctx")),
        P(("dp", "ctx"), "tensor"),
        P(("dp", "ctx"), "tensor"),
        P("tensor", ("dp", "ctx")),
        P(("dp", "ctx")),
    )
    return jax.shard_map(
        per_device, mesh=mesh, in_specs=in_specs, out_specs=out_specs, check_vma=False
    )
```

profile of v0, /device:TPU:0, one launch (start us, length us, event | category | flops | bytes accessed | tf_op | source)
XLA Modules:
  0.0 1710.6 jit_solution(8271007243975048578)
XLA Ops:
  13.2 10.2 all-reduce.5
  31.3 18.0 %all-gather = bf16[1,2048]{1,0:T(2,128)(2,1)S(1)} all-gather(bf16[1,256]{1,0:T(2,128)(2,1)S(1)} %convert_element_type.171), channel_id=2, replica_groups=mesh['dp'=4,'ctx'=8,'tensor'=4] {'ctx'}, dimensions={1}, use_global_device_ids=true | all-gather | bytes 4608 | tf_op jit(solution)/shard_map/all_gather | solution.py:60
  50.7 16.2 all-gather.6.cloned.1.call-done
  79.1 30.9 %all-gather.4.cloned.1.call-done = bf16[2048,512]{1,0:T(8,128)(2,1)} async-done(((bf16[256,512]{1,0:T(8,128)(2,1)}), bf16[2048,512]{1,0:T(8,128)(2,1)}) %all-gather.4.cloned.1.call-update) | async-done | bytes 2097168 | tf_op jit(solution)/shard_map/all_gather | solution.py:59
  119.2 58.2 %all-reduce.12.cloned.1.call-done = f32[256,2048]{1,0:T(8,128)} async-done(((f32[256,2048]{1,0:T(8,128)}), f32[256,2048]{1,0:T(8,128)}) %all-reduce.12.cloned.1.call-update) | async-done | bytes 2097168 | tf_op jit(solution)/shard_map/psum | solution.py:82
  195.3 58.1 %all-reduce.14.cloned.1.call-done = f32[256,2048]{1,0:T(8,128)} async-done(((f32[256,2048]{1,0:T(8,128)}), f32[256,2048]{1,0:T(8,128)}) %all-reduce.14.cloned.1.call-update) | async-done | bytes 2097168 | tf_op jit(solution)/shard_map/psum | solution.py:91
  257.7 8.0 multiply_convert_fusion.1
  268.2 7.2 convolution_add_fusion.2
  275.9 57.9 %all-reduce.16.cloned.1.call-done = f32[256,2048]{1,0:T(8,128)} async-done(((f32[256,2048]{1,0:T(8,128)}), f32[256,2048]{1,0:T(8,128)}) %all-reduce.16.cloned.1.call-update) | async-done | bytes 2097168 | tf_op jit(solution)/shard_map/psum | solution.py:109
  364.3 6.9 fusion.2
  384.2 31.7 %reduce-scatter.18.cloned.1.call-done = f32[256,512]{1,0:T(8,128)} async-done(((f32[2048,512]{1,0:T(8,128)}), f32[256,512]{1,0:T(8,128)}) %reduce-scatter.18.cloned.1.call-update) | async-done | bytes 524304 | tf_op jit(solution)/shard_map/reduce_scatter | solution.py:143
  417.3 9.8 all-reduce.4
  433.7 36.7 %reduce-scatter.20.cloned.1.call-done = f32[256,512]{0,1:T(8,128)} async-done(((f32[2048,512]{0,1:T(8,128)}), f32[256,512]{0,1:T(8,128)}) %reduce-scatter.20.cloned.1.call-update) | async-done | bytes 524304 | tf_op jit(solution)/shard_map/reduce_scatter | solution.py:149
  495.9 7.9 convolution_convert_fusion
  503.9 7.2 convolution_convert_fusion.1
  511.3 7.1 convolution_convert_fusion.2
  521.0 114.1 %reduce-scatter.22.cloned.1.call-done = bf16[512,64]{0,1:T(8,128)(2,1)} async-done(((bf16[512,2048]{0,1:T(8,128)(2,1)}), bf16[512,64]{0,1:T(8,128)(2,1)}) %reduce-scatter.22.cloned.1.call-update) | async-done | bytes 65552 | tf_op jit(solution)/shard_map/reduce_scatter | solution.py:207
  636.6 153.1 %all-reduce.6 = (bf16[4,128]{1,0:T(4,128)(2,1)S(1)}, bf16[4,128]{1,0:T(4,128)(2,1)S(1)}, bf16[2048]{0:T(1024)(128)(2,1)S(1)}, bf16[2048]{0:T(1024)(128)(2,1)S(1)}) all-reduce(bf16[4,128]{1,0:T(4,128)(2,1)S(1)} %bitcast.153, bf16[4,128]{1,0:T(4,128)(2,1)S(1)} %bitcast.154, ...), channel_id=9, replica_groups=mesh['dp'=4,'ctx'=8,'tensor'=4] {'dp','ctx'}, use_global_device_ids=true, to_apply=%region_26.27.clone | all-reduce | flops 5120 | bytes 20480
  795.5 49.6 %reduce-scatter.34.cloned.1.call-done = bf16[64,512]{1,0:T(8,128)(2,1)} async-done(((bf16[2048,512]{1,0:T(8,128)(2,1)}), bf16[64,512]{1,0:T(8,128)(2,1)}) %reduce-scatter.34.cloned.1.call-update) | async-done | bytes 65552
  846.8 160.1 %reduce-scatter.30.cloned.1.call-done = bf16[64,512]{1,0:T(8,128)(2,1)} async-done(((bf16[2048,512]{1,0:T(8,128)(2,1)}), bf16[64,512]{1,0:T(8,128)(2,1)}) %reduce-scatter.30.cloned.1.call-update) | async-done | bytes 65552
  1008.5 160.1 %reduce-scatter.32.cloned.1.call-done = bf16[64,512]{1,0:T(8,128)(2,1)} async-done(((bf16[2048,512]{1,0:T(8,128)(2,1)}), bf16[64,512]{1,0:T(8,128)(2,1)}) %reduce-scatter.32.cloned.1.call-update) | async-done | bytes 65552
  1170.4 175.9 %reduce-scatter.28.cloned.1.call-done = bf16[2048,64]{0,1:T(8,128)(2,1)} async-done(((bf16[2048,2048]{0,1:T(8,128)(2,1)}), bf16[2048,64]{0,1:T(8,128)(2,1)}) %reduce-scatter.28.cloned.1.call-update) | async-done | bytes 262160 | tf_op jit(solution)/shard_map/reduce_scatter | solution.py:225
  1348.0 176.3 %reduce-scatter.26.cloned.1.call-done = bf16[64,2048]{1,0:T(8,128)(2,1)} async-done(((bf16[2048,2048]{1,0:T(8,128)(2,1)}), bf16[64,2048]{1,0:T(8,128)(2,1)}) %reduce-scatter.26.cloned.1.call-update) | async-done | bytes 262160 | tf_op jit(solution)/shard_map/reduce_scatter | solution.py:222
  1526.1 176.0 %reduce-scatter.24.cloned.1.call-done = bf16[64,2048]{1,0:T(8,128)(2,1)} async-done(((bf16[2048,2048]{1,0:T(8,128)(2,1)}), bf16[64,2048]{1,0:T(8,128)(2,1)}) %reduce-scatter.24.cloned.1.call-update) | async-done | bytes 262160 | tf_op jit(solution)/shard_map/reduce_scatter | solution.py:219
  (181 shorter events, 157.7 us)
Async XLA Ops:
  7.2 59.7 %all-gather.6.cloned.1.call-start = ((), (), s32[]{:S(2)}) async-start(), calls=%async_computation.10 | async-start | bytes 2359296 | tf_op jit(solution)/shard_map/all_gather | solution.py:58
  11.7 11.7 copy-start.27
  25.2 84.8 %all-gather.4.cloned.1.call-start = ((), (), s32[]{:S(2)}) async-start(), calls=%async_computation.9 | async-start | bytes 2359296 | tf_op jit(solution)/shard_map/all_gather | solution.py:59
  28.3 149.1 %all-reduce.12.cloned.1.call-start = ((), (), s32[]{:S(2)}) async-start(), calls=%async_computation.11 | async-start | bytes 4194304 | tf_op jit(solution)/shard_map/psum | solution.py:82
  110.0 6.8 copy-start.17
  118.9 60.5 %copy-start.24 = (f32[2048]{0:T(1024)S(1)}, f32[2048]{0:T(1024)}, u32[]{:S(2)}) copy-start(f32[2048]{0:T(1024)} %param.22) | copy-start | bytes 24580
  118.9 134.5 %all-reduce.14.cloned.1.call-start = ((), (), s32[]{:S(2)}) async-start(), calls=%async_computation.12 | async-start | bytes 4194304 | tf_op jit(solution)/shard_map/psum | solution.py:91
  179.6 6.8 slice-start.6
  180.0 11.2 slice-start.2
  194.9 60.4 %copy-start.25 = (f32[2048]{0:T(1024)S(1)}, f32[2048]{0:T(1024)}, u32[]{:S(2)}) copy-start(f32[2048]{0:T(1024)} %param.26) | copy-start | bytes 24580
  195.0 138.9 %all-reduce.16.cloned.1.call-start = ((), (), s32[]{:S(2)}) async-start(), calls=%async_computation.13 | async-start | bytes 4194304 | tf_op jit(solution)/shard_map/psum | solution.py:109
  255.6 10.2 slice-start.4
  257.7 8.1 slice-start.5
  275.4 140.5 %reduce-scatter.18.cloned.1.call-start = ((), (), s32[]{:S(2)}) async-start(), calls=%async_computation.14 | async-start | bytes 4718592 | tf_op jit(solution)/shard_map/reduce_scatter | solution.py:143
  346.1 6.8 slice-start.1
  363.4 107.0 %reduce-scatter.20.cloned.1.call-start = ((), (), s32[]{:S(2)}) async-start(), calls=%async_computation.15 | async-start | bytes 4718592 | tf_op jit(solution)/shard_map/reduce_scatter | solution.py:149
  371.3 263.8 %reduce-scatter.22.cloned.1.call-start = ((), (), s32[]{:S(2)}) async-start(), calls=%async_computation.17 | async-start | bytes 2162688 | tf_op jit(solution)/shard_map/reduce_scatter | solution.py:207
  375.6 416.6 %all-reduce.18.cloned.1.call-start = ((), (), s32[]{:S(2)}) async-start(), calls=%async_computation.16 | async-start | bytes 2097152 | tf_op jit(solution)/shard_map/psum | solution.py:182
  474.5 370.5 %reduce-scatter.34.cloned.1.call-start = ((), (), s32[]{:S(2)}) async-start(), calls=%async_computation.23 | async-start | bytes 2162688
  481.6 525.2 %reduce-scatter.30.cloned.1.call-start = ((), (), s32[]{:S(2)}) async-start(), calls=%async_computation.21 | async-start | bytes 2162688
  488.7 680.0 %reduce-scatter.32.cloned.1.call-start = ((), (), s32[]{:S(2)}) async-start(), calls=%async_computation.22 | async-start | bytes 2162688
  494.7 851.5 %reduce-scatter.28.cloned.1.call-start = ((), (), s32[]{:S(2)}) async-start(), calls=%async_computation.20 | async-start | bytes 8650752 | tf_op jit(solution)/shard_map/reduce_scatter | solution.py:225
  503.8 1020.5 %reduce-scatter.26.cloned.1.call-start = ((), (), s32[]{:S(2)}) async-start(), calls=%async_computation.19 | async-start | bytes 8650752 | tf_op jit(solution)/shard_map/reduce_scatter | solution.py:222
  511.1 1191.0 %reduce-scatter.24.cloned.1.call-start = ((), (), s32[]{:S(2)}) async-start(), calls=%async_computation.18 | async-start | bytes 8650752 | tf_op jit(solution)/shard_map/reduce_scatter | solution.py:219
  (30 other events, 87.2 us)
Sparse Core Ops, SparseCore 0:
  25.3 41.5 all-gather.5
  69.1 40.8 all-gather.3
  119.0 58.3 all-reduce.11
  195.1 58.2 all-reduce.13
  275.5 58.2 all-reduce.15
  363.5 52.4 reduce-scatter.17
  418.5 51.8 reduce-scatter.19
  472.9 162.1 reduce-scatter.21
  638.2 41.4 all-reduce.17
  682.0 162.9 reduce-scatter.33
  847.4 159.3 reduce-scatter.29
  1009.2 159.4 reduce-scatter.31
  1171.1 175.1 reduce-scatter.27
  1348.5 175.7 reduce-scatter.25
  1526.6 175.4 reduce-scatter.23
where the time goes:
time: 1720 us; the launch traced here: 1710 us
  waiting for transfers between devices  1300 us (76%)
  blocking collectives  191 us (11%)
  matrix products  115 us (7%)
  local copies, waits for them, and re-layouts  44.9 us (3%)
  other arithmetic  40.3 us (2%)
    unnamed x18, waiting for transfers between devices  370 us
    reduce_scatter x1, waiting for transfers between devices, per_device(): lax.psum_scatter(local_grads[8].astype(jnp.bfloat16), ('dp', 'ctx'), scat...  176 us
    reduce_scatter x1, waiting for transfers between devices, per_device(): lax.psum_scatter(local_grads[7].astype(jnp.bfloat16), ('dp', 'ctx'), scat...  176 us
    reduce_scatter x1, waiting for transfers between devices, per_device(): lax.psum_scatter(local_grads[9].astype(jnp.bfloat16), ('dp', 'ctx'), scat...  176 us
    unnamed x1, blocking collectives  153 us
    reduce_scatter x1, waiting for transfers between devices, per_device(): lax.psum_scatter(local_grads[3].astype(jnp.bfloat16), ('dp', 'ctx'), scat...  114 us
    psum x1, waiting for transfers between devices, per_device(): lax.psum(jnp.dot(attended_low, w_out, preferred_element_type=jnp.float32)...  58.2 us
    psum x1, waiting for transfers between devices, per_device(): lax.psum(jnp.dot(mixed_low, w_down, preferred_element_type=jnp.float32),...  58.1 us
  transfers between devices with their start and end apart: 15, of which 14 were waited for; matrix products, arithmetic and copies ran while one was open for 6% of the time, Pallas kernels for 0%

commit v1 on v0

v1 whole, which is shorter than its diff:
```python
import functools
import jax
import jax.numpy as jnp
from jax import lax
from jax.experimental import pallas as pl
from jax.experimental.pallas import tpu as pltpu
from jax.sharding import PartitionSpec as P

MESH = pl.DeviceIdType.MESH
F32 = jnp.float32
BF16 = jnp.bfloat16
EPS = 1e-06
T = 256
D = 2048
HD = 128
OWN = 64
NC = 4
CW = D // NC
VMEM = pl.BlockSpec(memory_space=pltpu.VMEM)
ANY = pl.BlockSpec(memory_space=pl.ANY)


def place():
    t = lax.axis_index("tensor")
    ctx = lax.axis_index("ctx")
    return t // 2, lax.rem(t, 2), ctx // 4, lax.rem(ctx, 4)


def core_peer(yh, core):
    return {"tensor": yh * 2 + (1 - core)}


def far_peer(yh, core):
    return {"tensor": (1 - yh) * 2 + core}


def remote(src, dst, send_sem, recv_sem, device):
    return pltpu.make_async_remote_copy(
        src_ref=src,
        dst_ref=dst,
        send_sem=send_sem,
        recv_sem=recv_sem,
        device_id=device,
        device_id_type=MESH,
    )


def greet(devices):
    barrier = pltpu.get_barrier_semaphore()
    for device in devices:
        pl.semaphore_signal(barrier, inc=1, device_id=device, device_id_type=MESH)
    pl.semaphore_wait(barrier, len(devices))


def rows_of(index, count):
    return pl.ds(pl.multiple_of(index * count, count), count)


def reduce_rows(part, near, far, out_low, acc, sems):
    yh, core, _, _ = place()
    near_send, near_recv, far_send, far_recv = sems
    near_copies, far_copies = [], []
    for j in range(NC):
        cols = pl.ds(j * CW, CW)
        for slot, row in ((0, (1 - yh) * 2 + (1 - core)), (1, yh * 2 + (1 - core))):
            copy = remote(
                part.at[rows_of(row, OWN), cols],
                near.at[slot, :, cols],
                near_send.at[slot, j],
                near_recv.at[slot, j],
                core_peer(yh, core),
            )
            copy.start()
            near_copies.append(copy)
    for j in range(NC):
        cols = pl.ds(j * CW, CW)
        near_copies[2 * j].wait_recv()
        out_low[:, cols] = (
            part[rows_of((1 - yh) * 2 + core, OWN), cols].astype(F32)
            + near[0, :, cols].astype(F32)
        ).astype(BF16)
        copy = remote(
            out_low.at[:, cols], far.at[:, cols], far_send.at[j], far_recv.at[j], far_peer(yh, core)
        )
        copy.start()
        far_copies.append(copy)
    for j in range(NC):
        cols = pl.ds(j * CW, CW)
        near_copies[2 * j + 1].wait_recv()
        acc[:, cols] = part[rows_of(yh * 2 + core, OWN), cols].astype(F32) + near[
            1, :, cols
        ].astype(F32)
    for j in range(NC):
        cols = pl.ds(j * CW, CW)
        far_copies[j].wait_recv()
        acc[:, cols] = acc[:, cols] + far[:, cols].astype(F32)
    for copy in near_copies + far_copies:
        copy.wait_send()


def gather_rows(out, sems):
    yh, core, _, _ = place()
    own_send, own_recv, far_send, far_recv, on_send, on_recv = sems
    mine, other = rows_of(yh * 2 + core, OWN), rows_of((1 - yh) * 2 + core, OWN)
    far_copies, own_copies, on_copies = [], [], []
    for j in range(NC):
        block = out.at[mine, pl.ds(j * CW, CW)]
        copy = remote(block, block, far_send.at[j], far_recv.at[j], far_peer(yh, core))
        copy.start()
        far_copies.append(copy)
    for j in range(NC):
        block = out.at[mine, pl.ds(j * CW, CW)]
        copy = remote(block, block, own_send.at[j], own_recv.at[j], core_peer(yh, core))
        copy.start()
        own_copies.append(copy)
    for j in range(NC):
        far_copies[j].wait_recv()
        block = out.at[other, pl.ds(j * CW, CW)]
        copy = remote(block, block, on_send.at[j], on_recv.at[j], core_peer(yh, core))
        copy.start()
        on_copies.append(copy)
    for copy in own_copies + on_copies:
        copy.wait_recv()
    for copy in far_copies + own_copies + on_copies:
        copy.wait_send()


REDUCE_SCRATCH = [
    pltpu.VMEM((2, OWN, D), BF16),
    pltpu.VMEM((OWN, D), BF16),
    pltpu.VMEM((OWN, D), BF16),
    pltpu.VMEM((OWN, D), F32),
    pltpu.SemaphoreType.DMA((2, NC)),
    pltpu.SemaphoreType.DMA((2, NC)),
    pltpu.SemaphoreType.DMA((NC,)),
    pltpu.SemaphoreType.DMA((NC,)),
]
GATHER_SCRATCH = [pltpu.SemaphoreType.DMA((NC,))] * 6


def summed(part, near, far, out_low, acc, *sems):
    yh, core, _, _ = place()
    greet([core_peer(yh, core), far_peer(yh, core)])
    reduce_rows(part, near, far, out_low, acc, sems[:4])
    return rows_of(yh * 2 + core, OWN)


def norm_scale(v):
    return lax.rsqrt(jnp.mean(v * v, axis=1, keepdims=True) + EPS)


def norm_back(v, r, g, dy):
    column_sum = jnp.sum(dy * g * v, axis=1, keepdims=True)
    return r * g * dy - v * (r * r * r) * (column_sum / D)


def attn_out_kernel(part, features, gain, out, attn_own, hidden_own, *scratch):
    reduce, gather = scratch[:8], scratch[8:14]
    mine = summed(part, *reduce)
    v = reduce[3][...]
    hidden = features[mine, :].astype(F32) + v * norm_scale(v) * gain[...]
    out[mine, :] = hidden.astype(BF16)
    attn_own[...] = v
    hidden_own[...] = hidden
    gather_rows(out, gather)


def mlp_out_kernel(part, hidden_own, cotangent, gain, out, result_own, gain_grad, *scratch):
    reduce, gather = scratch[:8], scratch[8:14]
    mine = summed(part, *reduce)
    v = reduce[3][...]
    z = norm_scale(v)
    dy = cotangent[mine, :].astype(F32)
    g = gain[...]
    out[mine, :] = norm_back(v, z, g, dy).astype(BF16)
    result_own[...] = (hidden_own[...] + v * z * g).astype(BF16)
    gain_grad[...] = jnp.sum(dy * v * z, axis=0, keepdims=True)
    gather_rows(out, gather)


def mlp_back_kernel(part, attn_own, cotangent, gain, out, d_hidden_own, gain_grad, *scratch):
    reduce, gather = scratch[:8], scratch[8:14]
    mine = summed(part, *reduce)
    dy = cotangent[mine, :].astype(F32) + reduce[3][...]
    v = attn_own[...]
    a = norm_scale(v)
    g = gain[...]
    out[mine, :] = norm_back(v, a, g, dy).astype(BF16)
    d_hidden_own[...] = dy
    gain_grad[...] = jnp.sum(dy * v * a, axis=0, keepdims=True)
    gather_rows(out, gather)


def input_grad_kernel(part, d_hidden_own, out, *scratch):
    reduce, gather = scratch[:8], scratch[8:14]
    mine = summed(part, *reduce)
    out[mine, :] = (d_hidden_own[...] + reduce[3][...]).astype(BF16)
    gather_rows(out, gather)


def tensor_call(kernel, name, collective_id, operands, outs):
    return pl.pallas_call(
        kernel,
        name=name,
        out_shape=[jax.ShapeDtypeStruct(shape, kind) for shape, kind in outs],
        in_specs=[VMEM] * len(operands),
        out_specs=[VMEM] * len(outs),
        scratch_shapes=REDUCE_SCRATCH + GATHER_SCRATCH,
        compiler_params=pltpu.CompilerParams(
            collective_id=collective_id, has_side_effects=True, vmem_limit_bytes=24 * 2**20
        ),
    )(*operands)


def row_device(yl, x):
    return {"ctx": yl * 4 + x}


def all_peers(yh, core, yl, x):
    peers = [core_peer(yh, core), far_peer(yh, core)]
    peers += [row_device(yl, lax.rem(x + s, 4)) for s in (1, 2, 3)]
    peers += [row_device(1 - yl, lax.rem(x + s, 4)) for s in range(4)]
    return peers


def tensor_sum(own, near, far, send, recv):
    yh, core, _, _ = place()
    copy = remote(own.at[0], near, send.at[0], recv.at[0], core_peer(yh, core))
    copy.start()
    copy.wait_recv()
    own[1] = own[0] + near[...]
    again = remote(own.at[1], far, send.at[1], recv.at[1], far_peer(yh, core))
    again.start()
    again.wait_recv()
    total = own[1] + far[...]
    copy.wait_send()
    again.wait_send()
    return total


def two_columns(first, second):
    lane = lax.broadcasted_iota(jnp.int32, (T, HD), 1)
    return jnp.where(lane < HD // 2, first, second)


def dot(a, b, dims):
    return lax.dot_general(a, b, (dims, ((), ())), preferred_element_type=F32)


class Spread:
    def __init__(self, src, dst, sems):
        self.src, self.dst = src, dst
        self.send, self.recv, self.down_send, self.down_recv = sems

    def row_copy(self, s):
        _, _, yl, x = place()
        h = lax.rem(x + s, 4)
        return remote(
            self.src.at[:, pl.ds(pl.multiple_of(h * HD, HD), HD)],
            self.dst.at[rows_of(yl * 4 + x, T)],
            self.send.at[s],
            self.recv.at[s],
            row_device(yl, h),
        )

    def down_copy(self, s):
        _, _, yl, x = place()
        h = lax.rem(x + s, 4)
        return remote(
            self.src.at[:, pl.ds(pl.multiple_of(h * HD, HD), HD)],
            self.dst.at[rows_of(x, T)],
            self.down_send.at[s],
            self.down_recv.at[s],
            row_device(1, h),
        )


def keep_own(src, dst, block):
    _, _, _, x = place()
    dst[rows_of(block, T), :] = src[:, pl.ds(pl.multiple_of(x * HD, HD), HD)]


def attend_kernel(
    q_raw, k_raw, value, seg, q_gain, k_gain,
    attended, q_head, k_head, v_head, probs_out, scale_out,
    seg_all, q_low, k_low, sums, near, far, result,
    v_sems, k_sems, q_send, q_recv, s_send, s_recv, sum_send, sum_recv, a_send, a_recv,
):
    yh, core, yl, x = place()
    greet(all_peers(yh, core, yl, x))
    me = yl * 4 + x
    v_sems = [v_sems.at[i] for i in range(4)]
    k_sems = [k_sems.at[i] for i in range(4)]
    values = Spread(value, v_head, v_sems)
    keys = Spread(k_low, k_head, k_sems)

    @pl.when(yl == 0)
    def _():
        for s in range(4):
            values.down_copy(s).start()

    for s in (1, 2, 3):
        values.row_copy(s).start()
    seg_all[me] = jnp.broadcast_to(seg[...].astype(F32), (8, T))

    def seg_copy(s):
        dx, dy = s % 4, s // 4
        to = row_device(lax.rem(yl + dy, 2), lax.rem(x + dx, 4))
        return remote(seg_all.at[me], seg_all.at[me], s_send.at[s], s_recv.at[s], to)

    for s in range(1, 8):
        seg_copy(s).start()

    qr, kr = q_raw[...], k_raw[...]
    sums[0] = two_columns(
        jnp.sum(qr * qr, axis=1, keepdims=True), jnp.sum(kr * kr, axis=1, keepdims=True)
    )
    keep_own(value, v_head, me)
    scales = lax.rsqrt(tensor_sum(sums, near, far, sum_send, sum_recv) / D + EPS)
    scale_out[...] = scales
    k_low[...] = (kr * scales[:, HD // 2 : HD // 2 + 1] * k_gain[...]).astype(BF16)

    @pl.when(yl == 0)
    def _():
        for s in range(4):
            keys.down_copy(s).start()

    for s in (1, 2, 3):
        keys.row_copy(s).start()
    q_low[...] = (qr * scales[:, :1] * q_gain[...]).astype(BF16)

    def q_copy(s):
        h = lax.rem(x + s, 4)
        return remote(
            q_low.at[:, pl.ds(pl.multiple_of(h * HD, HD), HD)],
            q_head.at[rows_of(x, T)],
            q_send.at[s],
            q_recv.at[s],
            row_device(yl, h),
        )

    for s in (1, 2, 3):
        q_copy(s).start()
    keep_own(k_low, k_head, me)
    keep_own(q_low, q_head, x)
    for s in range(1, 8):
        seg_copy(s).wait()
    for s in (1, 2, 3):
        values.row_copy(s).wait()
        keys.row_copy(s).wait()
        q_copy(s).wait()

    @pl.when(yl == 0)
    def _():
        for s in range(4):
            values.down_copy(s).wait_send()
            keys.down_copy(s).wait_send()

    @pl.when(yl == 1)
    def _():
        for s in range(4):
            values.down_copy(s).wait_recv()
            keys.down_copy(s).wait_recv()

    lane = lax.broadcasted_iota(jnp.int32, (8, HD), 0)
    pick = jnp.where(lane == 0, 1.0, 0.0)

    def attend(row, i):
        blocks = row * 4 + i + 1
        width = blocks * T
        q = q_head[i * T : (i + 1) * T, :]
        scores = dot(q, k_head[:width, :], ((1,), (1,))) * HD ** (-0.5)
        own_seg = dot(seg_all[row * 4 + i], pick, ((0,), (0,)))[:, :1]
        seg_keys = jnp.concatenate([seg_all[b, :1, :] for b in range(blocks)], axis=1)
        q_place = lax.broadcasted_iota(jnp.int32, (T, width), 0) + (blocks - 1) * T
        k_place = lax.broadcasted_iota(jnp.int32, (T, width), 1)
        counted = (k_place <= q_place) & (seg_keys == own_seg)
        scores = jnp.where(counted, scores, -1e30)
        exps = jnp.exp(scores - jnp.max(scores, axis=1, keepdims=True))
        probs = (exps * (1.0 / jnp.sum(exps, axis=1, keepdims=True))).astype(BF16)
        probs_out[i, :, :width] = probs
        result[i] = dot(probs, v_head[:width, :], ((1,), (0,))).astype(BF16)

    def back_copy(i):
        return remote(
            result.at[i],
            attended.at[:, pl.ds(pl.multiple_of(x * HD, HD), HD)],
            a_send.at[i],
            a_recv.at[x],
            row_device(yl, i),
        )

    for i in range(4):
        for row in range(2):

            @pl.when(yl == row)
            def _():
                attend(row, i)

        @pl.when(x == i)
        def _():
            attended[:, i * HD : (i + 1) * HD] = result[i]

        @pl.when(x != i)
        def _():
            back_copy(i).start()

    for h in range(4):

        @pl.when(x != h)
        def _():
            back_copy(h).wait_send()
            remote(
                result.at[h],
                attended.at[:, h * HD : (h + 1) * HD],
                a_send.at[h],
                a_recv.at[h],
                row_device(yl, h),
            ).wait_recv()


def attend(q_raw, k_raw, value, seg, q_gain, k_gain):
    dma = pltpu.SemaphoreType.DMA
    operands = (q_raw, k_raw, value, seg, q_gain, k_gain)
    outs = [
        ((T, 4 * HD), BF16),
        ((4 * T, HD), BF16),
        ((8 * T, HD), BF16),
        ((8 * T, HD), BF16),
        ((4, T, 8 * T), BF16),
        ((T, HD), F32),
    ]
    return pl.pallas_call(
        attend_kernel,
        name="attend",
        out_shape=[jax.ShapeDtypeStruct(shape, kind) for shape, kind in outs],
        in_specs=[VMEM] * len(operands),
        out_specs=[VMEM] * len(outs),
        scratch_shapes=[
            pltpu.VMEM((8, 8, T), F32),
            pltpu.VMEM((T, 4 * HD), BF16),
            pltpu.VMEM((T, 4 * HD), BF16),
            pltpu.VMEM((2, T, HD), F32),
            pltpu.VMEM((T, HD), F32),
            pltpu.VMEM((T, HD), F32),
            pltpu.VMEM((4, T, HD), BF16),
            dma((4, 4)),
            dma((4, 4)),
            dma((4,)),
            dma((4,)),
            dma((8,)),
            dma((8,)),
            dma((2,)),
            dma((2,)),
            dma((4,)),
            dma((4,)),
        ],
        compiler_params=pltpu.CompilerParams(
            collective_id=5, has_side_effects=True, vmem_limit_bytes=40 * 2**20
        ),
    )(*operands)


def attend_back_kernel(
    d_attended, q_head, k_head, v_head, probs_in, q_raw, k_raw, scales_in, q_gain, k_gain,
    d_q_low, d_k_low, d_v_low, q_gain_grad, k_gain_grad,
    d_out, dq_send_buf, dk_send_buf, dv_send_buf, dk_acc, dv_acc, dq_got, dk_got, dv_got,
    sums, near, far,
    o_send, o_recv, dq_send, dq_recv, dk_send, dk_recv, dv_send, dv_recv, sum_send, sum_recv,
):
    yh, core, yl, x = place()
    greet(all_peers(yh, core, yl, x))
    scale = HD ** (-0.5)

    def o_copy(s):
        h = lax.rem(x + s, 4)
        return remote(
            d_attended.at[:, pl.ds(pl.multiple_of(h * HD, HD), HD)],
            d_out.at[rows_of(x, T)],
            o_send.at[s],
            o_recv.at[s],
            row_device(yl, h),
        )

    for s in (1, 2, 3):
        o_copy(s).start()
    keep_own(d_attended, d_out, x)
    dk_acc[...] = jnp.zeros_like(dk_acc)
    dv_acc[...] = jnp.zeros_like(dv_acc)
    for s in (1, 2, 3):
        o_copy(s).wait()

    def back(row, i):
        width = (row * 4 + i + 1) * T
        q = q_head[i * T : (i + 1) * T, :]
        do = d_out[i * T : (i + 1) * T, :]
        probs_low = probs_in[i, :, :width]
        probs = probs_low.astype(F32)
        d_probs = dot(do, v_head[:width, :], ((1,), (1,)))
        delta = jnp.sum(probs * d_probs, axis=1, keepdims=True)
        d_scores = (probs * (d_probs - delta)).astype(BF16)
        dq_send_buf[i] = (dot(d_scores, k_head[:width, :], ((1,), (0,))) * scale).astype(BF16)
        dk_acc[:width, :] += dot(d_scores, q, ((0,), (0,)))
        dv_acc[:width, :] += dot(probs_low, do, ((0,), (0,)))

    def dq_copy(i):
        return remote(
            dq_send_buf.at[i], dq_got.at[x], dq_send.at[i], dq_recv.at[x], row_device(yl, i)
        )

    for i in range(4):
        for row in range(2):

            @pl.when(yl == row)
            def _():
                back(row, i)

        @pl.when(x == i)
        def _():
            dq_got[i] = dq_send_buf[i]

        @pl.when(x != i)
        def _():
            dq_copy(i).start()

    def kv_copy(j, buf, got, send, recv):
        return remote(
            buf.at[j], got.at[yl, x], send.at[j], recv.at[yl, x], row_device(j // 4, j % 4)
        )

    dk_args = (dk_send_buf, dk_got, dk_send, dk_recv)
    dv_args = (dv_send_buf, dv_got, dv_send, dv_recv)
    for j in range(8):
        dk_send_buf[j] = (dk_acc[j * T : (j + 1) * T, :] * scale).astype(BF16)
        dv_send_buf[j] = dv_acc[j * T : (j + 1) * T, :].astype(BF16)
        here = (yl == j // 4) & (x == j % 4)

        @pl.when(here)
        def _():
            dk_got[j // 4, j % 4] = dk_send_buf[j]
            dv_got[j // 4, j % 4] = dv_send_buf[j]

        sends = (yl >= j // 4) & ~here

        @pl.when(sends)
        def _():
            kv_copy(j, *dk_args).start()
            kv_copy(j, *dv_args).start()

    for h in range(4):

        @pl.when(x != h)
        def _():
            dq_copy(h).wait_send()
            remote(
                dq_send_buf.at[h], dq_got.at[h], dq_send.at[h], dq_recv.at[h], row_device(yl, h)
            ).wait_recv()

        for row in range(2):
            comes = (row >= yl) & ~((yl == row) & (x == h))

            @pl.when(comes)
            def _():
                for buf, got, send, recv in (dk_args, dv_args):
                    remote(
                        buf.at[0],
                        got.at[row, h],
                        send.at[0],
                        recv.at[row, h],
                        row_device(row, h),
                    ).wait_recv()

    for j in range(8):
        here = (yl == j // 4) & (x == j % 4)
        sends = (yl >= j // 4) & ~here

        @pl.when(sends)
        def _():
            kv_copy(j, *dk_args).wait_send()
            kv_copy(j, *dv_args).wait_send()

    @pl.when(yl == 1)
    def _():
        for h in range(4):
            dk_got[0, h] = jnp.zeros((T, HD), BF16)
            dv_got[0, h] = jnp.zeros((T, HD), BF16)

    q_sum = jnp.zeros((T, 1), F32)
    k_sum = jnp.zeros((T, 1), F32)
    for h in range(4):
        cols = slice(h * HD, (h + 1) * HD)
        dq = dq_got[h].astype(F32)
        dk = dk_got[0, h].astype(F32) + dk_got[1, h].astype(F32)
        d_v_low[:, cols] = (dv_got[0, h].astype(F32) + dv_got[1, h].astype(F32)).astype(BF16)
        q_sum += jnp.sum(dq * q_raw[:, cols] * q_gain[:, cols], axis=1, keepdims=True)
        k_sum += jnp.sum(dk * k_raw[:, cols] * k_gain[:, cols], axis=1, keepdims=True)
    sums[0] = two_columns(q_sum, k_sum)
    total = tensor_sum(sums, near, far, sum_send, sum_recv)
    qs, ks = scales_in[:, :1], scales_in[:, HD // 2 : HD // 2 + 1]
    q_coef = qs * qs * qs * (total[:, :1] / D)
    k_coef = ks * ks * ks * (total[:, HD // 2 : HD // 2 + 1] / D)
    for h in range(4):
        cols = slice(h * HD, (h + 1) * HD)
        dq = dq_got[h].astype(F32)
        dk = dk_got[0, h].astype(F32) + dk_got[1, h].astype(F32)
        qr, kr = q_raw[:, cols], k_raw[:, cols]
        d_q_low[:, cols] = (qs * q_gain[:, cols] * dq - qr * q_coef).astype(BF16)
        d_k_low[:, cols] = (ks * k_gain[:, cols] * dk - kr * k_coef).astype(BF16)
        q_gain_grad[:, cols] = jnp.sum(dq * qr * qs, axis=0, keepdims=True)
        k_gain_grad[:, cols] = jnp.sum(dk * kr * ks, axis=0, keepdims=True)


def attend_back(d_attended, saved, q_raw, k_raw, scales, q_gain, k_gain):
    dma = pltpu.SemaphoreType.DMA
    operands = (d_attended, *saved, q_raw, k_raw, scales, q_gain, k_gain)
    outs = [
        ((T, 4 * HD), BF16),
        ((T, 4 * HD), BF16),
        ((T, 4 * HD), BF16),
        ((1, 4 * HD), F32),
        ((1, 4 * HD), F32),
    ]
    return pl.pallas_call(
        attend_back_kernel,
        name="attend_back",
        out_shape=[jax.ShapeDtypeStruct(shape, kind) for shape, kind in outs],
        in_specs=[VMEM] * len(operands),
        out_specs=[VMEM] * len(outs),
        scratch_shapes=[
            pltpu.VMEM((4 * T, HD), BF16),
            pltpu.VMEM((4, T, HD), BF16),
            pltpu.VMEM((8, T, HD), BF16),
            pltpu.VMEM((8, T, HD), BF16),
            pltpu.VMEM((8 * T, HD), F32),
            pltpu.VMEM((8 * T, HD), F32),
            pltpu.VMEM((4, T, HD), BF16),
            pltpu.VMEM((2, 4, T, HD), BF16),
            pltpu.VMEM((2, 4, T, HD), BF16),
            pltpu.VMEM((2, T, HD), F32),
            pltpu.VMEM((T, HD), F32),
            pltpu.VMEM((T, HD), F32),
            dma((4,)),
            dma((4,)),
            dma((4,)),
            dma((4,)),
            dma((8,)),
            dma((2, 4)),
            dma((8,)),
            dma((2, 4)),
            dma((2,)),
            dma((2,)),
        ],
        compiler_params=pltpu.CompilerParams(
            collective_id=6, has_side_effects=True, vmem_limit_bytes=40 * 2**20
        ),
    )(*operands)


X_GROUPS = [[0, 1, 2, 3], [4, 5, 6, 7]]
Y_GROUPS = [[0, 4], [1, 5], [2, 6], [3, 7]]


def grad_kernel(pairs, *refs):
    ins, out = refs[:-1], refs[-1]
    at = 0
    for n, (left, right, width) in enumerate(pairs):
        product = dot(ins[left][...], ins[right][...], ((0,), (0,))).astype(BF16)
        for y in range(2):
            for x in range(4):
                out[x, 0, y, :, at : at + width] = product[(y * 4 + x) * 64 : (y * 4 + x + 1) * 64]
        at += width


def partial_grads(name, lefts, rights, pairs):
    rows = 4 * T
    total = sum(width for _, _, width in pairs)
    n = len(lefts)
    in_specs = [pl.BlockSpec((rows, D // 4), lambda i: (0, i)) for _ in lefts]
    in_specs += [pl.BlockSpec(right.shape, lambda i: (0, 0)) for right in rights]
    return pl.pallas_call(
        functools.partial(grad_kernel, [(a, n + b, w) for a, b, w in pairs]),
        name=name,
        grid=(4,),
        out_shape=jax.ShapeDtypeStruct((4, 4, 2, 64, total), BF16),
        in_specs=in_specs,
        out_specs=pl.BlockSpec((4, 1, 2, 64, total), lambda i: (0, i, 0, 0, 0)),
        compiler_params=pltpu.CompilerParams(vmem_limit_bytes=40 * 2**20),
        cost_estimate=pl.CostEstimate(
            flops=2 * rows * D * total,
            bytes_accessed=2 * rows * (D * n + total) + 2 * D * total,
            transcendentals=0,
        ),
    )(*lefts, *rights)


def quarters(arrays):
    return jnp.concatenate(
        [a.reshape(T, 4, a.shape[1] // 4).transpose(1, 0, 2) for a in arrays], axis=2
    )


def over_dp(blocks):
    return lax.all_to_all(blocks, "dp", 0, 0, tiled=True)


def scatter_grads(partial):
    width = partial.shape[-1]
    got = lax.all_to_all(partial, "ctx", 0, 0, axis_index_groups=X_GROUPS, tiled=True)
    total = jnp.sum(got.astype(F32), axis=0).astype(BF16)
    swapped = lax.all_to_all(
        total.transpose(1, 0, 2, 3), "ctx", 0, 0, axis_index_groups=Y_GROUPS, tiled=True
    )
    total = jnp.sum(swapped.astype(F32), axis=0).astype(BF16)
    return over_dp(total).astype(F32).transpose(1, 0, 2)


def per_device(
    inputs, segments, w_query, w_key, w_value, w_out, q_gain, k_gain, attn_gain,
    w_gate, w_up, w_down, mlp_gain, cotangent,
):
    features, top = inputs[0], cotangent[0]
    q_row, k_row = q_gain.reshape(1, -1), k_gain.reshape(1, -1)
    a_row, m_row = attn_gain.reshape(1, -1), mlp_gain.reshape(1, -1)

    def matmul(a, w):
        return jnp.dot(a, w, preferred_element_type=F32)

    def matmul_t(a, w):
        return lax.dot_general(a, w, (((1,), (1,)), ((), ())), preferred_element_type=F32)

    q_raw = matmul(features, w_query)
    k_raw = matmul(features, w_key)
    value = matmul(features, w_value).astype(BF16)
    attended, *saved, scales = attend(q_raw, k_raw, value, segments, q_row, k_row)
    part = matmul(attended, w_out).astype(BF16)
    hidden_low, attn_own, hidden_own = tensor_call(
        attn_out_kernel, "attn_out", 1, (part, features, a_row),
        [((T, D), BF16), ((OWN, D), F32), ((OWN, D), F32)],
    )
    gate = matmul(hidden_low, w_gate)
    upward = matmul(hidden_low, w_up)
    sigma = jax.nn.sigmoid(gate)
    activated = gate * sigma
    mixed = (activated * upward).astype(BF16)
    part = matmul(mixed, w_down).astype(BF16)
    d_mlp_low, result_own, mlp_gain_grad = tensor_call(
        mlp_out_kernel, "mlp_out", 2, (part, hidden_own, top, m_row),
        [((T, D), BF16), ((OWN, D), BF16), ((1, D), F32)],
    )
    outputs = lax.all_gather(result_own, "tensor", axis=0, tiled=True)
    d_mixed = matmul_t(d_mlp_low, w_down)
    d_up = (d_mixed * activated).astype(BF16)
    d_gate = (d_mixed * upward * sigma * (1.0 + gate * (1.0 - sigma))).astype(BF16)
    part = (matmul_t(d_gate, w_gate) + matmul_t(d_up, w_up)).astype(BF16)
    d_attn_low, d_hidden_own, attn_gain_grad = tensor_call(
        mlp_back_kernel, "mlp_back", 3, (part, attn_own, top, a_row),
        [((T, D), BF16), ((OWN, D), F32), ((1, D), F32)],
    )
    d_attended = matmul_t(d_attn_low, w_out).astype(BF16)
    d_q, d_k, d_v, q_gain_grad, k_gain_grad = attend_back(
        d_attended, saved, q_raw, k_raw, scales, q_row, k_row
    )
    part = (matmul_t(d_q, w_query) + matmul_t(d_k, w_key) + matmul_t(d_v, w_value)).astype(BF16)
    (input_grad,) = tensor_call(
        input_grad_kernel, "input_grad", 4, (part, d_hidden_own), [((T, D), BF16)]
    )

    def gathered(a):
        return lax.all_gather(a, "dp", axis=0, tiled=True)

    hidden_all, top_all = gathered(hidden_low), gathered(d_mlp_low)
    features_all, attn_all = gathered(features), gathered(d_attn_low)
    right = over_dp(quarters([d_gate, d_up, mixed])).reshape(4 * T, 1536)
    mlp = partial_grads(
        "mlp_grads", [hidden_all, top_all], [right[:, :1024], right[:, 1024:]],
        [(0, 0, 1024), (1, 1, 512)],
    )
    mlp = scatter_grads(mlp)
    right = over_dp(quarters([d_q, d_k, d_v, attended])).reshape(4 * T, 512)
    proj = partial_grads(
        "attn_grads", [features_all, attn_all], [right[:, :384], right[:, 384:]],
        [(0, 0, 384), (1, 1, 128)],
    )
    proj = scatter_grads(proj)

    gains = jnp.stack([attn_gain_grad[0], mlp_gain_grad[0]])
    gains = lax.psum(gains, ("dp", "ctx", "tensor"))
    heads = lax.psum(jnp.stack([q_gain_grad[0], k_gain_grad[0]]), ("dp", "ctx"))
    rank = lax.axis_index("dp") * 8 + lax.axis_index("ctx")
    gains = lax.dynamic_slice_in_dim(gains, rank * 64, 64, 1)
    heads = lax.dynamic_slice_in_dim(heads.reshape(2, 4, HD), rank * 4, 4, 2)

    def joined(block):
        return block.reshape(64, -1)

    return (
        outputs[None],
        input_grad[None],
        joined(proj[:, :, :128]),
        joined(proj[:, :, 128:256]),
        joined(proj[:, :, 256:384]),
        joined(proj[:, :, 384:]).T,
        heads[0],
        heads[1],
        gains[0],
        joined(mlp[:, :, :512]),
        joined(mlp[:, :, 512:1024]),
        joined(mlp[:, :, 1024:]).T,
        gains[1],
    )


def solution(mesh):
    rows, full = P("dp", "ctx", None), P()
    down, across = P("tensor", None), P(None, "tensor")
    in_specs = (
        rows, P("dp", "ctx"), across, across, across, down, down, down, full,
        across, across, down, full, rows,
    )
    split = ("dp", "ctx")
    out_specs = (
        rows, rows, P(split, "tensor"), P(split, "tensor"), P(split, "tensor"), P("tensor", split),
        P("tensor", split), P("tensor", split), P(split), P(split, "tensor"), P(split, "tensor"),
        P("tensor", split), P(split),
    )
    return jax.shard_map(
        per_device, mesh=mesh, in_specs=in_specs, out_specs=out_specs, check_vma=False
    )
```

time: 1720 us -> 671 us (0.39)
  waiting for transfers between devices: 1300 us -> 193 us
  Pallas kernels: 0 us -> 178 us
  matrix products: 115 us -> 50.7 us
  blocking collectives: 191 us -> 142 us
  starting transfers between devices: 1.77 us -> 34.8 us
  other arithmetic: 40.3 us -> 12.9 us
    reduce_scatter x6 -> x0, waiting for transfers between devices: 711 us -> none  [the longest x1 176 us: per_device(): lax.psum_scatter(local_grads[8].astype(jnp.bfloat16), ('dp', 'ctx'), scat...]
    unnamed x18 -> x5, waiting for transfers between devices: 370 us -> 2.42 us
    pallas_call x0 -> x8, Pallas kernels: none -> 178 us  [the longest x4 94.2 us: tensor_call(): pl.pallas_call(kernel, name=name, out_shape=[jax.ShapeDtypeStruct(shape,...]
    psum x4 -> x0, waiting for transfers between devices: 174 us -> none  [the longest x1 58.2 us: per_device(): lax.psum(jnp.dot(attended_low, w_out, preferred_element_type=jnp.float32)...]
    unnamed x1 -> x0, blocking collectives: 153 us -> none
    all_to_all x0 -> x8, waiting for transfers between devices: none -> 148 us  [the longest x4 82.4 us: over_dp(): return lax.all_to_all(blocks, 'dp', 0, 0, tiled=True)]
    psum x2, blocking collectives: 19.9 us -> 142 us  [the longest x1 78.9 us: per_device(): heads = lax.psum(jnp.stack([q_gain_grad[0], k_gain_grad[0]]), ('dp', 'ctx'))]
    dot_general x27 -> x14, matrix products: 115 us -> 50.7 us  [the longest x7 29.2 us: matmul_t(): lax.dot_general(a, w, (((1,), (1,)), ((), ())), preferred_element_type=F32)]
  transfers between devices with their start and end apart: 15 -> 13, of which waited for: 14 -> 6; matrix products, arithmetic and copies ran while one was open for 6% -> 11% of each run, Pallas kernels for 0% -> 27%
where the time goes in v1:
time: 671 us; the launch traced here: 663 us
  waiting for transfers between devices  193 us (29%)
  Pallas kernels  178 us (27%)
  blocking collectives  142 us (21%)
  matrix products  50.7 us (8%)
  starting transfers between devices  34.8 us (5%)
  local copies, waits for them, and re-layouts  34.7 us (5%)
  between operations  16.6 us (2%)
  other arithmetic  12.9 us (2%)
    pallas_call x4, Pallas kernels, tensor_call(): pl.pallas_call(kernel, name=name, out_shape=[jax.ShapeDtypeStruct(shape,...  94.2 us
    all_to_all x4, waiting for transfers between devices, over_dp(): return lax.all_to_all(blocks, 'dp', 0, 0, tiled=True)  82.4 us
    psum x1, blocking collectives, per_device(): heads = lax.psum(jnp.stack([q_gain_grad[0], k_gain_grad[0]]), ('dp', 'ctx'))  78.9 us
    all_to_all x2, waiting for transfers between devices, scatter_grads(): lax.all_to_all(partial, 'ctx', 0, 0, axis_index_groups=X_GROUPS, tiled=True)  66 us
    psum x1, blocking collectives, per_device(): gains = lax.psum(gains, ('dp', 'ctx', 'tensor'))  63.3 us
    all_gather x4, waiting for transfers between devices, gathered(): return lax.all_gather(a, 'dp', axis=0, tiled=True)  42.5 us
    pallas_call x1, Pallas kernels, attend_back(): pl.pallas_call(attend_back_kernel, name='attend_back', out_shape=[jax.Sha...  35.1 us
    pallas_call x1, Pallas kernels, attend(): pl.pallas_call(attend_kernel, name='attend', out_shape=[jax.ShapeDtypeStr...  33.7 us
  transfers between devices with their start and end apart: 13, of which 6 were waited for; matrix products, arithmetic and copies ran while one was open for 11% of the time, Pallas kernels for 27%

profile of v1, /device:TPU:0, one launch (start us, length us, event | category | flops | bytes accessed | tf_op | source)
XLA Modules:
  0.0 663.0 jit_solution(9760271720550370489)
XLA Ops:
  14.0 33.7 %attend.1 = (bf16[256,512]{1,0:T(8,128)(2,1)S(1)}, bf16[1024,128]{1,0:T(8,128)(2,1)S(1)}, bf16[2048,128]{1,0:T(8,128)(2,1)S(1)}, bf16[2048,128]{1,0:T(8,128)(2,1...) custom-call(f32[256,512]{1,0:T(8,128)S(1)} %fusion.6.q_raw, f32[256,512]{1,0:T(8,128)S(1)} %fusion.4.k_raw, ...), custom_call_target="tpu_custom_call" | custom-call | tf_op jit(solution)/shard_map/attend/pallas_call | solution.py:433
  49.2 20.5 %attn_out.1 = (bf16[256,2048]{1,0:T(8,128)(2,1)S(1)}, f32[64,2048]{1,0:T(8,128)S(1)}, f32[64,2048]{1,0:T(8,128)S(1)}) custom-call(bf16[256,2048]{1,0:T(8,128)(2,1)S(1)} %convolution_convert_fusion.part, bf16[256,2048]{1,0:T(8,128)(2,1)S(1)} %bitcast.141, f32[1,2048]{1,0:T(1,128)S(1)} %bitcast.144), custom_call_target="tpu_custom_call" | custom-call | tf_op jit(solution)/shard_map/attn_out/pallas_call | solution.py:202
  72.3 6.2 fusion.8
  78.5 8.0 %multiply_convert_fusion.2 = (bf16[256,2048]{1,0:T(8,128)(2,1)S(1)}, f32[256,2048]{1,0:T(8,128)}) fusion(f32[256,2048]{1,0:T(8,128)S(1)} %fusion.8, bf16[256,2048]{1,0:T(8,128)(2,1)S(1)} %copy-done.13, bf16[2048,2048]{1,0:T(8,128)(2,1)} %param.24), kind=kOutput, calls=%fused_computation.10 | convolution fusion | flops 2150629376 | bytes 14680064 | tf_op jit(solution)/shard_map/dot_general | solution.py:726
  89.0 22.5 %mlp_out.1 = (bf16[256,2048]{1,0:T(8,128)(2,1)}, bf16[64,2048]{1,0:T(8,128)(2,1)}, f32[1,2048]{1,0:T(1,128)S(1)}) custom-call(bf16[256,2048]{1,0:T(8,128)(2,1)S(1)} %convolution_convert_fusion.1.part, f32[64,2048]{1,0:T(8,128)S(1)} %copy-done.31, bf16[256,2048]{1,0:T(8,128)(2,1)S(1)} %bitcast.139, f32[1,2048]{1,0:T(1,128)S(1)} %bitcast.146), custom_call_target="tpu_custom_call" | custom-call | tf_op jit(solution)/shard_map/mlp_out/pallas_call | solution.py:202
  111.5 7.7 %multiply_convert_fusion = (bf16[256,2048]{1,0:T(8,128)(2,1)S(1)}, bf16[256,2048]{1,0:T(8,128)(2,1)S(1)}) fusion(f32[256,2048]{1,0:T(8,128)} %copy-done.61, f32[256,2048]{1,0:T(8,128)} %get-tuple-element.67, bf16[256,2048]{1,0:T(8,128)(2,1)} %get-tuple-element.37, bf16[2048,2048]{1,0:T(8,128)(2,1)} %param.25), kind=kOutput, calls=%fused_computation.8 | convolution fusion | flops 2154299392 | bytes 15728640 | tf_op jit(solution)/shard_map/dot_general | solution.py:729
  119.3 6.7 %fusion.9 = f32[256,2048]{1,0:T(8,128)S(1)} fusion(bf16[256,2048]{1,0:T(8,128)(2,1)S(1)} %get-tuple-element.54, bf16[2048,2048]{1,0:T(8,128)(2,1)} %param.23), kind=kOutput, calls=%fused_computation.49 | convolution fusion | flops 2147483648 | bytes 11534336 | tf_op jit(solution)/shard_map/dot_general | solution.py:729
  126.0 5.8 fusion.part
  131.8 21.2 %mlp_back.1 = (bf16[256,2048]{1,0:T(8,128)(2,1)S(1)}, f32[64,2048]{1,0:T(8,128)S(1)}, f32[1,2048]{1,0:T(1,128)S(1)}) custom-call(bf16[256,2048]{1,0:T(8,128)(2,1)S(1)} %fusion.part, f32[64,2048]{1,0:T(8,128)S(1)} %copy-done.29, bf16[256,2048]{1,0:T(8,128)(2,1)S(1)} %bitcast.140, f32[1,2048]{1,0:T(1,128)S(1)} %bitcast.145), custom_call_target="tpu_custom_call" | custom-call | tf_op jit(solution)/shard_map/mlp_back/pallas_call | solution.py:202
  160.6 35.1 %attend_back.1 = (bf16[256,512]{1,0:T(8,128)(2,1)S(1)}, bf16[256,512]{1,0:T(8,128)(2,1)S(1)}, bf16[256,512]{1,0:T(8,128)(2,1)S(1)}, f32[1,512]{1,0:T(1,128)S(1)}, f32[1,512]{1,0:T(1,128)S(1)}) custom-call(bf16[256,512]{1,0:T(8,128)(2,1)S(1)} %convolution_convert_fusion.2.d_attended, bf16[1024,128]{1,0:T(8,128)(2,1)S(1)} %copy-done.33, ...), custom_call_target="tpu_custom_call" | custom-call | tf_op jit(solution)/shard_map/attend_back/pallas_call | solution.py:623
  197.6 4.8 all-to-all-start
  205.9 12.3 %all-to-all-done = bf16[4,256,512]{2,1,0:T(8,128)(2,1)S(1)} async-done(((bf16[4,256,512]{2,1,0:T(8,128)(2,1)}), bf16[4,256,512]{2,1,0:T(8,128)(2,1)S(1)}, u32[]{:S(2)}, u32[]{:S(2)}) %all-to-all-start) | async-done | bytes 1048608 | tf_op jit(solution)/shard_map/all_to_all | solution.py:703
  218.2 4.7 all-to-all-start.4
  227.4 5.6 attn_grads.1
  233.1 59.2 %all-to-all-done.4 = bf16[4,256,1536]{2,1,0:T(8,128)(2,1)} async-done(((bf16[4,256,1536]{2,1,0:T(8,128)(2,1)}), bf16[4,256,1536]{2,1,0:T(8,128)(2,1)}, u32[]{:S(2)}, u32[]{:S(2)}) %all-to-all-start.4) | async-done | bytes 3145760 | tf_op jit(solution)/shard_map/all_to_all | solution.py:703
  299.8 42.5 %all-gather.13.cloned.1.call-done.refs_1_ = bf16[1024,2048]{1,0:T(8,128)(2,1)} async-done(((bf16[256,2048]{1,0:T(8,128)(2,1)}), bf16[1024,2048]{1,0:T(8,128)(2,1)}) %all-gather.13.cloned.1.call-update) | async-done | bytes 4194320 | tf_op jit(solution)/shard_map/all_gather | solution.py:769
  346.7 9.1 %mlp_grads.1 = bf16[4,4,2,64,1536]{4,3,2,1,0:T(8,128)(2,1)} custom-call(bf16[1024,2048]{1,0:T(8,128)(2,1)S(1)} %copy-done.45, bf16[1024,2048]{1,0:T(8,128)(2,1)S(1)} %copy-done.46, bf16[1024,1024]{1,0:T(8,128)(2,1)S(1)} %slice.66.refs_2_, bf16[1024,512]{1,0:T(8,128)(2,1)S(1)} %slice.67.refs_3_), custom_call_target="tpu_custom_call" | custom-call | flops 6442450944 | bytes 17825792 | tf_op jit(solution)/shard_map/mlp_grads/pallas_call | solution.py:680
  355.8 5.4 all-to-all-start.5
  366.8 66.0 %all-to-all-done.5 = bf16[4,4,2,64,1536]{4,3,2,1,0:T(8,128)(2,1)} async-done(((bf16[4,4,2,64,1536]{4,3,2,1,0:T(8,128)(2,1)}), bf16[4,4,2,64,1536]{4,3,2,1,0:T(8,128)(2,1)}, u32[]{:S(2)}, u32[]{:S(2)}) %all-to-all-start.5) | async-done | bytes 6291488 | tf_op jit(solution)/shard_map/all_to_all | solution.py:708
  445.4 4.9 all-to-all-start.6
  452.8 29.9 %input_grad.1 = bf16[256,2048]{1,0:T(8,128)(2,1)S(1)} custom-call(bf16[256,2048]{1,0:T(8,128)(2,1)S(1)} %fusion.1.part, f32[64,2048]{1,0:T(8,128)S(1)} %copy-done.23), custom_call_target="tpu_custom_call" | custom-call | tf_op jit(solution)/shard_map/input_grad/pallas_call | solution.py:202
  482.8 78.9 %psum.14 = f32[2,4,128]{2,1,0:T(4,128)S(1)} all-reduce(f32[2,4,128]{2,1,0:T(4,128)S(1)} %reshape.102), channel_id=1, replica_groups=mesh['dp'=4,'ctx'=8,'tensor'=4] {'dp','ctx'}, use_global_device_ids=true, to_apply=%region_2.0 | all-reduce | flops 1024 | bytes 8192 | tf_op jit(solution)/shard_map/psum | solution.py:788
  561.7 63.3 %psum.15 = f32[2,2048]{1,0:T(2,128)S(1)} all-reduce(f32[2,2048]{1,0:T(2,128)S(1)} %pad_maximum_fusion.2), channel_id=1, replica_groups=mesh['dp'=4,'ctx'=8,'tensor'=4] {'dp','ctx','tensor'}, use_global_device_ids=true, to_apply=%region_3.0 | all-reduce | flops 4096 | bytes 32768 | tf_op jit(solution)/shard_map/psum | solution.py:787
  643.0 7.6 %all-to-all-done.7 = bf16[4,64,1536]{2,1,0:T(8,128)(2,1)S(1)} async-done(((bf16[4,64,1536]{2,1,0:T(8,128)(2,1)}), bf16[4,64,1536]{2,1,0:T(8,128)(2,1)S(1)}, u32[]{:S(2)}, u32[]{:S(2)}) %all-to-all-start.7) | async-done | bytes 786464 | tf_op jit(solution)/shard_map/all_to_all | solution.py:703
  (197 shorter events, 84.8 us)
Async XLA Ops:
  8.0 40.4 %copy-start = (bf16[512,2048]{1,0:T(8,128)(2,1)S(1)}, bf16[512,2048]{1,0:T(8,128)(2,1)}, u32[]{:S(2)}) copy-start(bf16[512,2048]{1,0:T(8,128)(2,1)} %param.19) | copy-start | bytes 6291460
  8.0 215.0 %all-gather.15.cloned.1.call-start = ((), (), s32[]{:S(2)}) async-start(), calls=%async_computation.12 | async-start | bytes 5242880 | tf_op jit(solution)/shard_map/all_gather | solution.py:769
  8.8 214.3 %all-gather.9.cloned.1.call-start = ((), (), s32[]{:S(2)}) async-start(), calls=%async_computation.9 | async-start | bytes 5242880 | tf_op jit(solution)/shard_map/all_gather | solution.py:769
  13.2 34.5 %copy-start.8 = (f32[256,512]{1,0:T(8,128)}, f32[256,512]{1,0:T(8,128)S(1)}, u32[]{:S(2)}) copy-start(f32[256,512]{1,0:T(8,128)S(1)} %fusion.6.q_raw) | copy-start | bytes 1572868
  14.0 35.2 %copy-start.10 = (f32[256,512]{1,0:T(8,128)}, f32[256,512]{1,0:T(8,128)S(1)}, u32[]{:S(2)}) copy-start(f32[256,512]{1,0:T(8,128)S(1)} %fusion.4.k_raw) | copy-start | bytes 1572868
  14.0 35.2 %copy-start.34 = (f32[2048]{0:T(1024)S(1)}, f32[2048]{0:T(1024)}, u32[]{:S(2)}) copy-start(f32[2048]{0:T(1024)} %param.22) | copy-start | bytes 24580
  155.5 144.3 %all-gather.11.cloned.1.call-start = ((), (), s32[]{:S(2)}) async-start(), calls=%async_computation.10 | async-start | bytes 5242880 | tf_op jit(solution)/shard_map/all_gather | solution.py:769
  156.2 186.1 %all-gather.13.cloned.1.call-start = ((), (), s32[]{:S(2)}) async-start(), calls=%async_computation.11 | async-start | bytes 5242880 | tf_op jit(solution)/shard_map/all_gather | solution.py:769
  160.6 35.1 %copy-start.19 = (bf16[256,512]{1,0:T(8,128)(2,1)S(1)}, bf16[256,512]{1,0:T(8,128)(2,1)}, u32[]{:S(2)}) copy-start(bf16[256,512]{1,0:T(8,128)(2,1)} %copy-done.18) | copy-start | bytes 786436
  197.6 20.6 %all-to-all-start = ((bf16[4,256,512]{2,1,0:T(8,128)(2,1)}), bf16[4,256,512]{2,1,0:T(8,128)(2,1)S(1)}, u32[]{:S(2)}, u32[]{:S(2)}) async-start(bf16[4,256,512]{2,1,0:T(8,128)(2,1)} %pad_maximum_fusion.1), calls=%async_computation | async-start | bytes 2097152 | tf_op jit(solution)/shard_map/all_to_all | solution.py:703
  218.2 74.1 %all-to-all-start.4 = ((bf16[4,256,1536]{2,1,0:T(8,128)(2,1)}), bf16[4,256,1536]{2,1,0:T(8,128)(2,1)}, u32[]{:S(2)}, u32[]{:S(2)}) async-start(bf16[4,256,1536]{2,1,0:T(8,128)(2,1)} %pad_maximum_fusion), calls=%async_computation.4 | async-start | bytes 6291456 | tf_op jit(solution)/shard_map/all_to_all | solution.py:703
  292.3 63.6 %all-to-all-start.1 = ((bf16[4,4,2,64,512]{4,3,2,1,0:T(8,128)(2,1)}), bf16[4,4,2,64,512]{4,3,2,1,0:T(8,128)(2,1)}, u32[]{:S(2)}, u32[]{:S(2)}) async-start(bf16[4,4,2,64,512]{4,3,2,1,0:T(8,128)(2,1)} %attn_grads.1), calls=%async_computation.1 | async-start | bytes 4194304 | tf_op jit(solution)/shard_map/all_to_all | solution.py:708
  355.8 77.0 %all-to-all-start.5 = ((bf16[4,4,2,64,1536]{4,3,2,1,0:T(8,128)(2,1)}), bf16[4,4,2,64,1536]{4,3,2,1,0:T(8,128)(2,1)}, u32[]{:S(2)}, u32[]{:S(2)}) async-start(bf16[4,4,2,64,1536]{4,3,2,1,0:T(8,128)(2,1)} %mlp_grads.1), calls=%async_computation.5 | async-start | bytes 12582912 | tf_op jit(solution)/shard_map/all_to_all | solution.py:708
  361.2 279.0 %all-gather.7.cloned.1.call-start = ((), (), s32[]{:S(2)}) async-start(), calls=%async_computation.8 | async-start | bytes 1310720 | tf_op jit(solution)/shard_map/all_gather | solution.py:750
  363.9 72.4 %copy-start.17 = (bf16[256,512]{1,0:T(8,128)(2,1)S(1)}, bf16[256,512]{1,0:T(8,128)(2,1)}, u32[]{:S(2)}) copy-start(bf16[256,512]{1,0:T(8,128)(2,1)} %copy-done.16) | copy-start | bytes 786436
  363.9 72.4 %copy-start.47 = (f32[256,2048]{1,0:T(8,128)S(1)}, f32[256,2048]{1,0:T(8,128)}, u32[]{:S(2)}) copy-start(f32[256,2048]{1,0:T(8,128)} %fusion.10) | copy-start | bytes 6291460
  432.8 12.6 %all-to-all-start.2 = ((bf16[2,4,64,512]{3,2,1,0:T(8,128)(2,1)}), bf16[2,4,64,512]{3,2,1,0:T(8,128)(2,1)S(1)}, u32[]{:S(2)}, u32[]{:S(2)}) async-start(bf16[2,4,64,512]{3,2,1,0:T(8,128)(2,1)} %copy.59), calls=%async_computation.2 | async-start | bytes 1048576 | tf_op jit(solution)/shard_map/all_to_all | solution.py:710
  445.4 180.5 %all-to-all-start.6 = ((bf16[2,4,64,1536]{3,2,1,0:T(8,128)(2,1)}), bf16[2,4,64,1536]{3,2,1,0:T(8,128)(2,1)}, u32[]{:S(2)}, u32[]{:S(2)}) async-start(bf16[2,4,64,1536]{3,2,1,0:T(8,128)(2,1)} %copy.67), calls=%async_computation.6 | async-start | bytes 3145728 | tf_op jit(solution)/shard_map/all_to_all | solution.py:710
  452.7 30.0 %copy-start.41 = (f32[1,512]{1,0:T(1,128)S(1)}, f32[1,512]{1,0:T(1,128)}, u32[]{:S(2)}) copy-start(f32[1,512]{1,0:T(1,128)} %copy-done.40) | copy-start | bytes 6148
  452.7 30.0 %copy-start.43 = (f32[1,512]{1,0:T(1,128)S(1)}, f32[1,512]{1,0:T(1,128)}, u32[]{:S(2)}) copy-start(f32[1,512]{1,0:T(1,128)} %copy-done.42) | copy-start | bytes 6148
  452.8 108.9 %copy-start.39 = (f32[1,2048]{1,0:T(1,128)S(1)}, f32[1,2048]{1,0:T(1,128)}, u32[]{:S(2)}) copy-start(f32[1,2048]{1,0:T(1,128)} %copy-done.38) | copy-start | bytes 24580
  452.8 172.3 %copy-start.53 = (bf16[2,4,64,512]{3,2,1,0:T(8,128)(2,1)S(1)}, bf16[2,4,64,512]{3,2,1,0:T(8,128)(2,1)}, u32[]{:S(2)}) copy-start(bf16[2,4,64,512]{3,2,1,0:T(8,128)(2,1)} %copy-done.52) | copy-start | bytes 1572868
  626.0 10.1 %all-to-all-start.3 = ((bf16[4,64,512]{2,1,0:T(8,128)(2,1)}), bf16[4,64,512]{2,1,0:T(8,128)(2,1)S(1)}, u32[]{:S(2)}, u32[]{:S(2)}) async-start(bf16[4,64,512]{2,1,0:T(8,128)(2,1)} %reduce_sum.49), calls=%async_computation.3 | async-start | bytes 524288 | tf_op jit(solution)/shard_map/all_to_all | solution.py:703
  636.0 14.5 %all-to-all-start.7 = ((bf16[4,64,1536]{2,1,0:T(8,128)(2,1)}), bf16[4,64,1536]{2,1,0:T(8,128)(2,1)S(1)}, u32[]{:S(2)}, u32[]{:S(2)}) async-start(bf16[4,64,1536]{2,1,0:T(8,128)(2,1)} %reduce_sum.51), calls=%async_computation.7 | async-start | bytes 1572864 | tf_op jit(solution)/shard_map/all_to_all | solution.py:703
  (53 other events, 226.4 us)
Sparse Core Ops, SparseCore 0:
  10.5 50.9 all-gather.14
  155.6 50.1 all-gather.8
  208.0 82.1 all-gather.10
  291.7 50.5 all-gather.12
Sparse Core Ops, SparseCore 1:
  363.3 21.3 all-gather.6

commit v2 on v1

--- a/solution.py
+++ b/solution.py
@@ -26,12 +26,22 @@
     return t // 2, lax.rem(t, 2), ctx // 4, lax.rem(ctx, 4)
 
 
-def core_peer(yh, core):
-    return {"tensor": yh * 2 + (1 - core)}
-
-
-def far_peer(yh, core):
-    return {"tensor": (1 - yh) * 2 + core}
+def peer(dz=0, dy=0, dx=0, dh=0, dc=0):
+    yh, core, yl, x = place()
+    z = lax.rem(lax.axis_index("dp") + dz, 4)
+    ctx = lax.rem(yl + dy, 2) * 4 + lax.rem(x + dx, 4)
+    return {"dp": z, "ctx": ctx, "tensor": lax.rem(yh + dh, 2) * 2 + lax.rem(core + dc, 2)}
+
+
+CORE, FAR = (0, 0, 0, 0, 1), (0, 0, 0, 1, 0)
+
+
+def along(axis, s):
+    return (s, 0, 0, 0, 0) if axis == "z" else (0, 0, s, 0, 0)
+
+
+def spot(axis):
+    return lax.axis_index("dp") if axis == "z" else place()[3]
 
 
 def remote(src, dst, send_sem, recv_sem, device):
@@ -45,15 +55,157 @@
     )
 
 
-def greet(devices):
+def greet(offsets):
     barrier = pltpu.get_barrier_semaphore()
-    for device in devices:
-        pl.semaphore_signal(barrier, inc=1, device_id=device, device_id_type=MESH)
-    pl.semaphore_wait(barrier, len(devices))
+    for offset in offsets:
+        pl.semaphore_signal(barrier, inc=1, device_id=peer(*offset), device_id_type=MESH)
+    pl.semaphore_wait(barrier, len(offsets))
 
 
 def rows_of(index, count):
     return pl.ds(pl.multiple_of(index * count, count), count)
+
+
+class Move:
+    def __init__(self, source, shape, offsets, pairs):
+        self.source, self.shape, self.offsets, self.pairs = source, shape, offsets, pairs
+
+    def scratch(self):
+        dma = pltpu.SemaphoreType.DMA
+        return [dma((len(self.offsets),)), dma((len(self.offsets),)), dma((1,))]
+
+    def copies(self, src, dst, send, recv, local):
+        made = []
+        at = 0
+        for a, b, offset in self.pairs(src, dst):
+            if offset is None:
+                made.append(pltpu.make_async_copy(a, b, local.at[0]))
+            else:
+                made.append(remote(a, b, send.at[at], recv.at[at], peer(*offset)))
+                at += 1
+        return made
+
+
+def half_move(a, axis):
+    half = a.shape[1] // 2
+    offsets = [along(axis, s) for s in (1, 2, 3)]
+
+    def pairs(src, dst):
+        mine = src.at[:, pl.ds(pl.multiple_of(place()[1] * half, half), half)]
+        me = spot(axis)
+        return [(mine, dst.at[me], offset) for offset in offsets + [None]]
+
+    return Move(a, (4, T, half), offsets, pairs)
+
+
+def core_move(a):
+    return Move(a, a.shape, [CORE], lambda src, dst: [(src, dst, CORE)])
+
+
+def quarter_move(b, axis):
+    width = b.shape[1] // 4
+    offsets = [along(axis, s) for s in (1, 2, 3)]
+
+    def pairs(src, dst):
+        me = spot(axis)
+
+        def part(s):
+            return src.at[:, pl.ds(pl.multiple_of(lax.rem(me + s, 4) * width, width), width)]
+
+        made = [(part(s), dst.at[me], along(axis, s)) for s in (1, 2, 3)]
+        return made + [(part(0), dst.at[me], None)]
+
+    return Move(b, (4, T, width), offsets, pairs)
+
+
+def full_move(b, axis):
+    offsets = [along(axis, s) for s in (1, 2, 3)]
+
+    def pairs(src, dst):
+        return [(src, dst.at[spot(axis)], offset) for offset in offsets + [None]]
+
+    return Move(b, (4,) + b.shape, offsets, pairs)
+
+
+def block_move(p, axis):
+    offsets = [along(axis, s) for s in (1, 2, 3)]
+
+    def pairs(src, dst):
+        me = spot(axis)
+        made = [(src.at[lax.rem(me + s, 4)], dst.at[me], along(axis, s)) for s in (1, 2, 3)]
+        return made + [(src.at[me], dst.at[me], None)]
+
+    return Move(p, p.shape, offsets, pairs)
+
+
+def final_move(p, axis):
+    steps = [(dy, s) for dy in range(2) for s in range(4) if dy or s]
+
+    def offset(dy, s):
+        return (s, dy, 0, 0, 0) if axis == "z" else (0, dy, s, 0, 0)
+
+    def pairs(src, dst):
+        yl, me = place()[2], spot(axis)
+        made = [
+            (src.at[lax.rem(yl + dy, 2), lax.rem(me + s, 4)], dst.at[yl, me], offset(dy, s))
+            for dy, s in steps
+        ]
+        return made + [(src.at[yl, me], dst.at[yl, me], None)]
+
+    return Move(p, p.shape, [offset(*step) for step in steps], pairs)
+
+
+def rank_move(p):
+    steps = [(dz, dy, dx, 0, 0) for dz in range(4) for dy in range(2) for dx in range(4)][1:]
+
+    def pairs(src, dst):
+        _, _, yl, x = place()
+        z = lax.axis_index("dp")
+        me = z * 8 + yl * 4 + x
+
+        def rank(dz, dy, dx, *_):
+            return lax.rem(z + dz, 4) * 8 + lax.rem(yl + dy, 2) * 4 + lax.rem(x + dx, 4)
+
+        made = [(src.at[rank(*step)], dst.at[me], step) for step in steps]
+        return made + [(src.at[me], dst.at[me], None)]
+
+    return Move(p, p.shape, steps, pairs)
+
+
+def call(main, name, collective_id, operands, outs, scratch, offsets, moves, vmem):
+    n_in, n_out, n_move, n_scratch = len(operands), len(outs), len(moves), len(scratch)
+    offsets = list(dict.fromkeys(offsets + [o for move in moves for o in move.offsets]))
+
+    def kernel(*refs):
+        ins, rest = refs[:n_in], refs[n_in:]
+        sources, rest = rest[:n_move], rest[n_move:]
+        results, rest = rest[:n_out], rest[n_out:]
+        targets, rest = rest[:n_move], rest[n_move:]
+        own, sems = rest[:n_scratch], rest[n_scratch:]
+        greet(offsets)
+        copies = []
+        for i, move in enumerate(moves):
+            copies += move.copies(sources[i], targets[i], *sems[3 * i : 3 * i + 3])
+        for copy in copies:
+            copy.start()
+        if main is not None:
+            main(*ins, *results, *own)
+        for copy in copies:
+            copy.wait()
+
+    move_outs = [(move.shape, move.source.dtype) for move in moves]
+    got = pl.pallas_call(
+        kernel,
+        name=name,
+        out_shape=[jax.ShapeDtypeStruct(shape, kind) for shape, kind in outs + move_outs],
+        in_specs=[VMEM] * n_in + [ANY] * n_move,
+        out_specs=[VMEM] * n_out + [ANY] * n_move,
+        scratch_shapes=scratch + [s for move in moves for s in move.scratch()],
+        compiler_params=pltpu.CompilerParams(
+            collective_id=collective_id, has_side_effects=True, vmem_limit_bytes=vmem * 2**20
+        ),
+    )(*operands, *[move.source for move in moves])
+    return got[:n_out], got[n_out:]
 
 
 def reduce_rows(part, near, far, out_low, acc, sems):
@@ -68,7 +220,7 @@
                 near.at[slot, :, cols],
                 near_send.at[slot, j],
                 near_recv.at[slot, j],
-                core_peer(yh, core),
+                peer(*CORE),
             )
             copy.start()
             near_copies.append(copy)
@@ -80,7 +232,7 @@
             + near[0, :, cols].astype(F32)
         ).astype(BF16)
         copy = remote(
-            out_low.at[:, cols], far.at[:, cols], far_send.at[j], far_recv.at[j], far_peer(yh, core)
+            out_low.at[:, cols], far.at[:, cols], far_send.at[j], far_recv.at[j], peer(*FAR)
         )
         copy.start()
         far_copies.append(copy)
@@ -105,18 +257,18 @@
     far_copies, own_copies, on_copies = [], [], []
     for j in range(NC):
         block = out.at[mine, pl.ds(j * CW, CW)]
-        copy = remote(block, block, far_send.at[j], far_recv.at[j], far_peer(yh, core))
+        copy = remote(block, block, far_send.at[j], far_recv.at[j], peer(*FAR))
         copy.start()
         far_copies.append(copy)
     for j in range(NC):
         block = out.at[mine, pl.ds(j * CW, CW)]
-        copy = remote(block, block, own_send.at[j], own_recv.at[j], core_peer(yh, core))
+        copy = remote(block, block, own_send.at[j], own_recv.at[j], peer(*CORE))
         copy.start()
         own_copies.append(copy)
     for j in range(NC):
         far_copies[j].wait_recv()
         block = out.at[other, pl.ds(j * CW, CW)]
-        copy = remote(block, block, on_send.at[j], on_recv.at[j], core_peer(yh, core))
+        copy = remote(block, block, on_send.at[j], on_recv.at[j], peer(*CORE))
         copy.start()
         on_copies.append(copy)
     for copy in own_copies + on_copies:
@@ -140,7 +292,6 @@
 
 def summed(part, near, far, out_low, acc, *sems):
     yh, core, _, _ = place()
-    greet([core_peer(yh, core), far_peer(yh, core)])
     reduce_rows(part, near, far, out_low, acc, sems[:4])
     return rows_of(yh * 2 + core, OWN)
 
@@ -174,11 +325,13 @@
     g = gain[...]
     out[mine, :] = norm_back(v, z, g, dy).astype(BF16)
     result_own[...] = (hidden_own[...] + v * z * g).astype(BF16)
-    gain_grad[...] = jnp.sum(dy * v * z, axis=0, keepdims=True)
+    gain_grad[...] = jnp.broadcast_to(jnp.sum(dy * v * z, axis=0, keepdims=True), (8, D))
     gather_rows(out, gather)
 
 
-def mlp_back_kernel(part, attn_own, cotangent, gain, out, d_hidden_own, gain_grad, *scratch):
+def mlp_back_kernel(
+    part, attn_own, cotangent, gain, mlp_gain_grad, out, d_hidden_own, gain_grad, *scratch
+):
     reduce, gather = scratch[:8], scratch[8:14]
     mine = summed(part, *reduce)
     dy = cotangent[mine, :].astype(F32) + reduce[3][...]
@@ -187,7 +340,9 @@
     g = gain[...]
     out[mine, :] = norm_back(v, a, g, dy).astype(BF16)
     d_hidden_own[...] = dy
-    gain_grad[...] = jnp.sum(dy * v * a, axis=0, keepdims=True)
+    row = lax.broadcasted_iota(jnp.int32, (8, D), 0)
+    attn_grad = jnp.sum(dy * v * a, axis=0, keepdims=True)
+    gain_grad[...] = jnp.where(row == 0, attn_grad, mlp_gain_grad[...])
     gather_rows(out, gather)
 
 
@@ -198,38 +353,25 @@
     gather_rows(out, gather)
 
 
-def tensor_call(kernel, name, collective_id, operands, outs):
-    return pl.pallas_call(
-        kernel,
-        name=name,
-        out_shape=[jax.ShapeDtypeStruct(shape, kind) for shape, kind in outs],
-        in_specs=[VMEM] * len(operands),
-        out_specs=[VMEM] * len(outs),
-        scratch_shapes=REDUCE_SCRATCH + GATHER_SCRATCH,
-        compiler_params=pltpu.CompilerParams(
-            collective_id=collective_id, has_side_effects=True, vmem_limit_bytes=24 * 2**20
-        ),
-    )(*operands)
+def tensor_call(kernel, name, collective_id, operands, outs, moves):
+    scratch = REDUCE_SCRATCH + GATHER_SCRATCH
+    return call(kernel, name, collective_id, operands, outs, scratch, [CORE, FAR], moves, 24)
 
 
 def row_device(yl, x):
     return {"ctx": yl * 4 + x}
 
 
-def all_peers(yh, core, yl, x):
-    peers = [core_peer(yh, core), far_peer(yh, core)]
-    peers += [row_device(yl, lax.rem(x + s, 4)) for s in (1, 2, 3)]
-    peers += [row_device(1 - yl, lax.rem(x + s, 4)) for s in range(4)]
-    return peers
+ATTEND_PEERS = [CORE, FAR] + [(0, dy, dx, 0, 0) for dy in range(2) for dx in range(4) if dy or dx]
 
 
 def tensor_sum(own, near, far, send, recv):
     yh, core, _, _ = place()
-    copy = remote(own.at[0], near, send.at[0], recv.at[0], core_peer(yh, core))
+    copy = remote(own.at[0], near, send.at[0], recv.at[0], peer(*CORE))
     copy.start()
     copy.wait_recv()
     own[1] = own[0] + near[...]
-    again = remote(own.at[1], far, send.at[1], recv.at[1], far_peer(yh, core))
+    again = remote(own.at[1], far, send.at[1], recv.at[1], peer(*FAR))
     again.start()
     again.wait_recv()
     total = own[1] + far[...]
@@ -287,7 +429,6 @@
     v_sems, k_sems, q_send, q_recv, s_send, s_recv, sum_send, sum_recv, a_send, a_recv,
 ):
     yh, core, yl, x = place()
-    greet(all_peers(yh, core, yl, x))
     me = yl * 4 + x
     v_sems = [v_sems.at[i] for i in range(4)]
     k_sems = [k_sems.at[i] for i in range(4)]
@@ -419,7 +560,7 @@
             ).wait_recv()
 
 
-def attend(q_raw, k_raw, value, seg, q_gain, k_gain):
+def attend(q_raw, k_raw, value, seg, q_gain, k_gain, moves):
     dma = pltpu.SemaphoreType.DMA
     operands = (q_raw, k_raw, value, seg, q_gain, k_gain)
     outs = [
@@ -430,13 +571,7 @@
         ((4, T, 8 * T), BF16),
         ((T, HD), F32),
     ]
-    return pl.pallas_call(
-        attend_kernel,
-        name="attend",
-        out_shape=[jax.ShapeDtypeStruct(shape, kind) for shape, kind in outs],
-        in_specs=[VMEM] * len(operands),
-        out_specs=[VMEM] * len(outs),
-        scratch_shapes=[
+    scratch = [
             pltpu.VMEM((8, 8, T), F32),
             pltpu.VMEM((T, 4 * HD), BF16),
             pltpu.VMEM((T, 4 * HD), BF16),
@@ -454,22 +589,19 @@
             dma((2,)),
             dma((4,)),
             dma((4,)),
-        ],
-        compiler_params=pltpu.CompilerParams(
-            collective_id=5, has_side_effects=True, vmem_limit_bytes=40 * 2**20
-        ),
-    )(*operands)
+    ]
+    return call(attend_kernel, "attend", 5, operands, outs, scratch, ATTEND_PEERS, moves, 40)
 
 
 def attend_back_kernel(
-    d_attended, q_head, k_head, v_head, probs_in, q_raw, k_raw, scales_in, q_gain, k_gain,
-    d_q_low, d_k_low, d_v_low, q_gain_grad, k_gain_grad,
+    d_attended, q_head, k_head, v_head, probs_in, q_raw, k_raw, scales_in, q_gain, k_gain, gains,
+    d_q_low, d_k_low, d_v_low, q_gain_grad, k_gain_grad, gains_out,
     d_out, dq_send_buf, dk_send_buf, dv_send_buf, dk_acc, dv_acc, dq_got, dk_got, dv_got,
     sums, near, far,
     o_send, o_recv, dq_send, dq_recv, dk_send, dk_recv, dv_send, dv_recv, sum_send, sum_recv,
+    gain_near, gain_far, gain_sum, gain_send, gain_recv,
 ):
     yh, core, yl, x = place()
-    greet(all_peers(yh, core, yl, x))
     scale = HD ** (-0.5)
 
     def o_copy(s):
@@ -484,11 +616,18 @@
 
     for s in (1, 2, 3):
         o_copy(s).start()
+    gain_near_copy = remote(gains, gain_near, gain_send.at[0], gain_recv.at[0], peer(*CORE))
+    gain_near_copy.start()
     keep_own(d_attended, d_out, x)
     dk_acc[...] = jnp.zeros_like(dk_acc)
     dv_acc[...] = jnp.zeros_like(dv_acc)
     for s in (1, 2, 3):
         o_copy(s).wait()
+
+    gain_near_copy.wait()
+    gain_sum[...] = gains[...] + gain_near[...]
+    gain_far_copy = remote(gain_sum, gain_far, gain_send.at[1], gain_recv.at[1], peer(*FAR))
+    gain_far_copy.start()
 
     def back(row, i):
         width = (row * 4 + i + 1) * T
@@ -585,6 +724,8 @@
             dk_got[0, h] = jnp.zeros((T, HD), BF16)
             dv_got[0, h] = jnp.zeros((T, HD), BF16)
 
+    gain_far_copy.wait()
+    gains_out[...] = gain_sum[...] + gain_far[...]
     q_sum = jnp.zeros((T, 1), F32)
     k_sum = jnp.zeros((T, 1), F32)
     for h in range(4):
@@ -610,23 +751,18 @@
         k_gain_grad[:, cols] = jnp.sum(dk * kr * ks, axis=0, keepdims=True)
 
 
-def attend_back(d_attended, saved, q_raw, k_raw, scales, q_gain, k_gain):
+def attend_back(d_attended, saved, q_raw, k_raw, scales, q_gain, k_gain, gains, moves):
     dma = pltpu.SemaphoreType.DMA
-    operands = (d_attended, *saved, q_raw, k_raw, scales, q_gain, k_gain)
+    operands = (d_attended, *saved, q_raw, k_raw, scales, q_gain, k_gain, gains)
     outs = [
         ((T, 4 * HD), BF16),
         ((T, 4 * HD), BF16),
         ((T, 4 * HD), BF16),
         ((1, 4 * HD), F32),
         ((1, 4 * HD), F32),
+        ((8, D), F32),
     ]
-    return pl.pallas_call(
-        attend_back_kernel,
-        name="attend_back",
-        out_shape=[jax.ShapeDtypeStruct(shape, kind) for shape, kind in outs],
-        in_specs=[VMEM] * len(operands),
-        out_specs=[VMEM] * len(outs),
-        scratch_shapes=[
+    scratch = [
             pltpu.VMEM((4 * T, HD), BF16),
             pltpu.VMEM((4, T, HD), BF16),
             pltpu.VMEM((8, T, HD), BF16),
@@ -649,69 +785,82 @@
             dma((2, 4)),
             dma((2,)),
             dma((2,)),
-        ],
-        compiler_params=pltpu.CompilerParams(
-            collective_id=6, has_side_effects=True, vmem_limit_bytes=40 * 2**20
+            pltpu.VMEM((8, D), F32),
+            pltpu.VMEM((8, D), F32),
+            pltpu.VMEM((8, D), F32),
+            dma((2,)),
+            dma((2,)),
+    ]
+    return call(
+        attend_back_kernel, "attend_back", 6, operands, outs, scratch, ATTEND_PEERS, moves, 40
+    )
+
+
+def grad_kernel(layout, core_ref, own_half, other_half, *refs):
+    rights, out = refs[:-1], refs[-1]
+    ours = pl.program_id(0) // 2 == core_ref[0]
+
+    def product(left):
+        at = 0
+        for right in rights:
+            width = right.shape[2]
+            got = dot(
+                left[...].reshape(4 * T, D // 4), right[...].reshape(4 * T, width), ((0,), (0,))
+            ).astype(BF16)
+            for y in range(2):
+                for x in range(4):
+                    rows = got[(y * 4 + x) * 64 : (y * 4 + x + 1) * 64]
+                    if layout == "x":
+                        out[x, y, 0, :, at : at + width] = rows
+                    else:
+                        out[0, y, x, :, at : at + width] = rows
+            at += width
+
+    @pl.when(ours)
+    def _():
+        product(own_half)
+
+    @pl.when(jnp.logical_not(ours))
+    def _():
+        product(other_half)
+
+
+def partial_grads(name, layout, own_half, other_half, rights):
+    total = sum(right.shape[2] for right in rights)
+    core = lax.rem(lax.axis_index("tensor"), 2).reshape(1)
+    block = (4, T, D // 4)
+    in_specs = [
+        pl.BlockSpec(block, lambda i, c: (0, 0, jnp.where(i // 2 == c[0], i % 2, 0))),
+        pl.BlockSpec(block, lambda i, c: (0, 0, jnp.where(i // 2 == c[0], 0, i % 2))),
+    ]
+    in_specs += [pl.BlockSpec(right.shape, lambda i, c: (0, 0, 0)) for right in rights]
+    if layout == "x":
+        shape, out_block = (4, 2, 4, 64, total), (4, 2, 1, 64, total)
+        out_spec = pl.BlockSpec(out_block, lambda i, c: (0, 0, i, 0, 0))
+    else:
+        shape, out_block = (4, 2, 4, 64, total), (1, 2, 4, 64, total)
+        out_spec = pl.BlockSpec(out_block, lambda i, c: (i, 0, 0, 0, 0))
+    return pl.pallas_call(
+        functools.partial(grad_kernel, layout),
+        name=name,
+        grid_spec=pltpu.PrefetchScalarGridSpec(
+            num_scalar_prefetch=1, grid=(4,), in_specs=in_specs, out_specs=out_spec
         ),
-    )(*operands)
-
-
-X_GROUPS = [[0, 1, 2, 3], [4, 5, 6, 7]]
-Y_GROUPS = [[0, 4], [1, 5], [2, 6], [3, 7]]
-
-
-def grad_kernel(pairs, *refs):
-    ins, out = refs[:-1], refs[-1]
-    at = 0
-    for n, (left, right, width) in enumerate(pairs):
-        product = dot(ins[left][...], ins[right][...], ((0,), (0,))).astype(BF16)
-        for y in range(2):
-            for x in range(4):
-                out[x, 0, y, :, at : at + width] = product[(y * 4 + x) * 64 : (y * 4 + x + 1) * 64]
-        at += width
-
-
-def partial_grads(name, lefts, rights, pairs):
-    rows = 4 * T
-    total = sum(width for _, _, width in pairs)
-    n = len(lefts)
-    in_specs = [pl.BlockSpec((rows, D // 4), lambda i: (0, i)) for _ in lefts]
-    in_specs += [pl.BlockSpec(right.shape, lambda i: (0, 0)) for right in rights]
-    return pl.pallas_call(
-        functools.partial(grad_kernel, [(a, n + b, w) for a, b, w in pairs]),
-        name=name,
-        grid=(4,),
-        out_shape=jax.ShapeDtypeStruct((4, 4, 2, 64, total), BF16),
-        in_specs=in_specs,
-        out_specs=pl.BlockSpec((4, 1, 2, 64, total), lambda i: (0, i, 0, 0, 0)),
+        out_shape=jax.ShapeDtypeStruct(shape, BF16),
         compiler_params=pltpu.CompilerParams(vmem_limit_bytes=40 * 2**20),
         cost_estimate=pl.CostEstimate(
-            flops=2 * rows * D * total,
-            bytes_accessed=2 * rows * (D * n + total) + 2 * D * total,
+            flops=8 * T * D * total, bytes_accessed=8 * T * (D + total) + 2 * D * total,
             transcendentals=0,
         ),
-    )(*lefts, *rights)
-
-
-def quarters(arrays):
-    return jnp.concatenate(
-        [a.reshape(T, 4, a.shape[1] // 4).transpose(1, 0, 2) for a in arrays], axis=2
-    )
-
-
-def over_dp(blocks):
-    return lax.all_to_all(blocks, "dp", 0, 0, tiled=True)
-
-
-def scatter_grads(partial):
-    width = partial.shape[-1]
-    got = lax.all_to_all(partial, "ctx", 0, 0, axis_index_groups=X_GROUPS, tiled=True)
-    total = jnp.sum(got.astype(F32), axis=0).astype(BF16)
-    swapped = lax.all_to_all(
-        total.transpose(1, 0, 2, 3), "ctx", 0, 0, axis_index_groups=Y_GROUPS, tiled=True
-    )
-    total = jnp.sum(swapped.astype(F32), axis=0).astype(BF16)
-    return over_dp(total).astype(F32).transpose(1, 0, 2)
+    )(core, own_half, other_half, *rights)
+
+
+def add_up(blocks):
+    return jnp.sum(blocks.astype(F32), axis=0)
+
+
+def rows_out(final):
+    return add_up(final).transpose(1, 0, 2)
 
 
 def per_device(
@@ -731,11 +880,12 @@
     q_raw = matmul(features, w_query)
     k_raw = matmul(features, w_key)
     value = matmul(features, w_value).astype(BF16)
-    attended, *saved, scales = attend(q_raw, k_raw, value, segments, q_row, k_row)
+    (attended, *saved, scales), _ = attend(q_raw, k_raw, value, segments, q_row, k_row, [])
     part = matmul(attended, w_out).astype(BF16)
-    hidden_low, attn_own, hidden_own = tensor_call(
+    (hidden_low, attn_own, hidden_own), (features_half, attended_all) = tensor_call(
         attn_out_kernel, "attn_out", 1, (part, features, a_row),
         [((T, D), BF16), ((OWN, D), F32), ((OWN, D), F32)],
+        [half_move(features, "x"), full_move(attended, "z")],
     )
     gate = matmul(hidden_low, w_gate)
     upward = matmul(hidden_low, w_up)
@@ -743,52 +893,66 @@
     activated = gate * sigma
     mixed = (activated * upward).astype(BF16)
     part = matmul(mixed, w_down).astype(BF16)
-    d_mlp_low, result_own, mlp_gain_grad = tensor_call(
+    (d_mlp_low, result_own, gain_rows), (hidden_half, features_rest) = tensor_call(
         mlp_out_kernel, "mlp_out", 2, (part, hidden_own, top, m_row),
-        [((T, D), BF16), ((OWN, D), BF16), ((1, D), F32)],
+        [((T, D), BF16), ((OWN, D), BF16), ((8, D), F32)],
+        [half_move(hidden_low, "z"), core_move(features_half)],
     )
     outputs = lax.all_gather(result_own, "tensor", axis=0, tiled=True)
     d_mixed = matmul_t(d_mlp_low, w_down)
     d_up = (d_mixed * activated).astype(BF16)
     d_gate = (d_mixed * upward * sigma * (1.0 + gate * (1.0 - sigma))).astype(BF16)
     part = (matmul_t(d_gate, w_gate) + matmul_t(d_up, w_up)).astype(BF16)
-    d_attn_low, d_hidden_own, attn_gain_grad = tensor_call(
-        mlp_back_kernel, "mlp_back", 3, (part, attn_own, top, a_row),
-        [((T, D), BF16), ((OWN, D), F32), ((1, D), F32)],
+    (d_attn_low, d_hidden_own, gain_rows), (hidden_rest, gate_right, up_right) = tensor_call(
+        mlp_back_kernel, "mlp_back", 3, (part, attn_own, top, a_row, gain_rows),
+        [((T, D), BF16), ((OWN, D), F32), ((8, D), F32)],
+        [core_move(hidden_half), quarter_move(d_gate, "z"), quarter_move(d_up, "z")],
     )
     d_attended = matmul_t(d_attn_low, w_out).astype(BF16)
-    d_q, d_k, d_v, q_gain_grad, k_gain_grad = attend_back(
-        d_attended, saved, q_raw, k_raw, scales, q_row, k_row
-    )
+    mlp_in = partial_grads("mlp_in", "x", hidden_half, hidden_rest, [gate_right, up_right])
+    (d_q, d_k, d_v, q_gain_grad, k_gain_grad, gain_rows), moved = attend_back(
+        d_attended, saved, q_raw, k_raw, scales, q_row, k_row, gain_rows,
+        [
+            block_move(mlp_in, "x"), half_move(d_mlp_low, "z"), quarter_move(mixed, "z"),
+            quarter_move(d_attn_low, "z"),
+        ],
+    )
+    mlp_in, top_half, mixed_right, attn_left = moved
     part = (matmul_t(d_q, w_query) + matmul_t(d_k, w_key) + matmul_t(d_v, w_value)).astype(BF16)
-    (input_grad,) = tensor_call(
-        input_grad_kernel, "input_grad", 4, (part, d_hidden_own), [((T, D), BF16)]
-    )
-
-    def gathered(a):
-        return lax.all_gather(a, "dp", axis=0, tiled=True)
-
-    hidden_all, top_all = gathered(hidden_low), gathered(d_mlp_low)
-    features_all, attn_all = gathered(features), gathered(d_attn_low)
-    right = over_dp(quarters([d_gate, d_up, mixed])).reshape(4 * T, 1536)
-    mlp = partial_grads(
-        "mlp_grads", [hidden_all, top_all], [right[:, :1024], right[:, 1024:]],
-        [(0, 0, 1024), (1, 1, 512)],
-    )
-    mlp = scatter_grads(mlp)
-    right = over_dp(quarters([d_q, d_k, d_v, attended])).reshape(4 * T, 512)
-    proj = partial_grads(
-        "attn_grads", [features_all, attn_all], [right[:, :384], right[:, 384:]],
-        [(0, 0, 384), (1, 1, 128)],
-    )
-    proj = scatter_grads(proj)
-
-    gains = jnp.stack([attn_gain_grad[0], mlp_gain_grad[0]])
-    gains = lax.psum(gains, ("dp", "ctx", "tensor"))
-    heads = lax.psum(jnp.stack([q_gain_grad[0], k_gain_grad[0]]), ("dp", "ctx"))
-    rank = lax.axis_index("dp") * 8 + lax.axis_index("ctx")
-    gains = lax.dynamic_slice_in_dim(gains, rank * 64, 64, 1)
-    heads = lax.dynamic_slice_in_dim(heads.reshape(2, 4, HD), rank * 4, 4, 2)
+    out_grad = lax.dot_general(
+        attn_left.reshape(4 * T, 512), attended_all.reshape(4 * T, 512), (((0,), (0,)), ((), ())),
+        preferred_element_type=F32,
+    ).astype(BF16)
+    mlp_in = add_up(mlp_in).astype(BF16)
+    (input_grad,), moved = tensor_call(
+        input_grad_kernel, "input_grad", 4, (part, d_hidden_own), [((T, D), BF16)],
+        [
+            quarter_move(d_q, "x"), quarter_move(d_k, "x"), quarter_move(d_v, "x"),
+            core_move(top_half), final_move(mlp_in, "z"),
+            final_move(out_grad.reshape(2, 4, 64, 512), "x"),
+        ],
+    )
+    *qkv_right, top_rest, mlp_in, out_grad = moved
+    qkv = partial_grads("qkv", "z", features_half, features_rest, qkv_right)
+    mlp_down = partial_grads("mlp_down", "x", top_half, top_rest, [mixed_right])
+    heads = jnp.stack([q_gain_grad, k_gain_grad]).reshape(2, 4, 32, 4).transpose(2, 0, 1, 3)
+    tiles = jnp.zeros((32, 8, HD), F32)
+    tiles = tiles.at[:, 0:2, :64].set(gain_rows[:2].reshape(2, 32, 64).transpose(1, 0, 2))
+    tiles = tiles.at[:, 2:4, :16].set(heads.reshape(32, 2, 16))
+    _, (qkv, mlp_down, tiles) = call(
+        None, "scatter", 7, (), [], [], [],
+        [block_move(qkv, "z"), block_move(mlp_down, "x"), rank_move(tiles)], 16,
+    )
+    _, (qkv, mlp_down) = call(
+        None, "place", 8, (), [], [], [],
+        [
+            final_move(add_up(qkv).astype(BF16), "x"),
+            final_move(add_up(mlp_down).astype(BF16), "z"),
+        ], 16,
+    )
+    gains = add_up(tiles)
+    qkv, mlp_in, mlp_down = rows_out(qkv), rows_out(mlp_in), rows_out(mlp_down)
+    out_grad = add_up(out_grad.reshape(8, 64, 512))
 
     def joined(block):
         return block.reshape(64, -1)
@@ -796,17 +960,17 @@
     return (
         outputs[None],
         input_grad[None],
-        joined(proj[:, :, :128]),
-        joined(proj[:, :, 128:256]),
-        joined(proj[:, :, 256:384]),
-        joined(proj[:, :, 384:]).T,
-        heads[0],
-        heads[1],
-        gains[0],
-        joined(mlp[:, :, :512]),
-        joined(mlp[:, :, 512:1024]),
-        joined(mlp[:, :, 1024:]).T,
-        gains[1],
+        joined(qkv[:, :, :128]),
+        joined(qkv[:, :, 128:256]),
+        joined(qkv[:, :, 256:]),
+        out_grad.T,
+        gains[2, :16].reshape(4, 4),
+        gains[3, :16].reshape(4, 4),
+        gains[0, :64],
+        joined(mlp_in[:, :, :512]),
+        joined(mlp_in[:, :, 512:]),
+        joined(mlp_down).T,
+        gains[1, :64],
     )
 
 

time: 671 us -> 424 us (0.63)
  waiting for transfers between devices: 193 us -> 0.02 us
  blocking collectives: 142 us -> 0 us
  Pallas kernels: 178 us -> 297 us
  starting transfers between devices: 34.8 us -> 0.04 us
  local copies, waits for them, and re-layouts: 34.7 us -> 46.9 us
    all_to_all x8 -> x0, waiting for transfers between devices: 148 us -> none  [the longest x4 82.4 us: over_dp(): return lax.all_to_all(blocks, 'dp', 0, 0, tiled=True)]
    psum x2 -> x0, blocking collectives: 142 us -> none  [the longest x1 78.9 us: per_device(): heads = lax.psum(jnp.stack([q_gain_grad[0], k_gain_grad[0]]), ('dp', 'ctx'))]
    pallas_call x8 -> x11, Pallas kernels: 178 us -> 297 us  [the longest x8 283 us: call(): pl.pallas_call(kernel, name=name, out_shape=[jax.ShapeDtypeStruct(shape,...]
    all_gather x4 -> x0, waiting for transfers between devices: 42.5 us -> none  [gathered(): return lax.all_gather(a, 'dp', axis=0, tiled=True)]
    all_to_all x8 -> x0, starting transfers between devices: 34.6 us -> none  [the longest x4 16.4 us: over_dp(): return lax.all_to_all(blocks, 'dp', 0, 0, tiled=True)]
    unnamed x132 -> x162, local copies, waits for them, and re-layouts: 22.5 us -> 38.3 us
  transfers between devices with their start and end apart: 13 -> 1, of which waited for: 6 -> 0; matrix products, arithmetic and copies ran while one was open for 11% -> 12% of each run, Pallas kernels for 27% -> 50%
where the time goes in v2:
time: 424 us; the launch traced here: 417 us
  Pallas kernels  297 us (70%)
  local copies, waits for them, and re-layouts  46.9 us (11%)
  matrix products  46.6 us (11%)
  between operations  15.3 us (4%)
  other arithmetic  10.5 us (2%)
    pallas_call x8, Pallas kernels, call(): pl.pallas_call(kernel, name=name, out_shape=[jax.ShapeDtypeStruct(shape,...  283 us
    unnamed x162, local copies, waits for them, and re-layouts  38.3 us
    dot_general x7, matrix products, matmul_t(): lax.dot_general(a, w, (((1,), (1,)), ((), ())), preferred_element_type=F32)  27.5 us
    dot_general x7, matrix products, matmul(): return jnp.dot(a, w, preferred_element_type=F32)  17.6 us
    pallas_call x3, Pallas kernels, partial_grads(): pl.pallas_call(functools.partial(grad_kernel, layout), name=name, grid_sp...  14.5 us
    reduce_sum x8, other arithmetic, add_up(): return jnp.sum(blocks.astype(F32), axis=0)  9.14 us
  transfers between devices with their start and end apart: 1, of which 0 were waited for; matrix products, arithmetic and copies ran while one was open for 12% of the time, Pallas kernels for 50%

profile of v2, /device:TPU:0, one launch (start us, length us, event | category | flops | bytes accessed | tf_op | source)
XLA Modules:
  0.0 416.7 jit_solution(992046958380426084)
XLA Ops:
  7.3 2.8 fusion.5.refs_1_.refs_6_
  12.8 33.7 %attend.1 = (bf16[256,512]{1,0:T(8,128)(2,1)S(1)}, bf16[1024,128]{1,0:T(8,128)(2,1)S(1)}, bf16[2048,128]{1,0:T(8,128)(2,1)S(1)}, bf16[2048,128]{1,0:T(8,128)(2,1...) custom-call(f32[256,512]{1,0:T(8,128)S(1)} %fusion.7.refs_0_.refs_5_, ...), custom_call_target="tpu_custom_call" | custom-call | tf_op jit(solution)/shard_map/attend/pallas_call | solution.py:197
  47.2 29.4 %attn_out.1 = (bf16[256,2048]{1,0:T(8,128)(2,1)S(1)}, f32[64,2048]{1,0:T(8,128)S(1)}, f32[64,2048]{1,0:T(8,128)S(1)}, bf16[4,256,1024]{2,1,0:T(8,128)(2,1)S(1)}, bf16[4,256,512]{2,1,0:T(8,128)(2,1)S(1)}) custom-call(bf16[256,2048]{1,0:T(8,128)(2,1)S(1)} %convolution_convert_fusion.refs_0_, bf16[256,2048]{1,0:T(8,128)(2,1)S(1)} %bitcast.84, ...), custom_call_target="tpu_custom_call" | custom-call | tf_op jit(solution)/shard_map/attn_out/pallas_call | solution.py:197
  78.5 2.3 fusion.9
  80.8 8.1 %multiply_convert_fusion.2 = (bf16[256,2048]{1,0:T(8,128)(2,1)S(1)}, f32[256,2048]{1,0:T(8,128)}) fusion(f32[256,2048]{1,0:T(8,128)S(1)} %fusion.9, bf16[256,2048]{1,0:T(8,128)(2,1)S(1)} %get-tuple-element.82.refs_4_, bf16[2048,2048]{1,0:T(8,128)(2,1)} %param.28), kind=kOutput, calls=%fused_computation.10 | convolution fusion | flops 2150629376 | bytes 14680064 | tf_op jit(solution)/shard_map/dot_general | solution.py:875
  89.0 2.3 convolution_convert_fusion.1.refs_0_
  91.4 27.2 %mlp_out.1 = (bf16[256,2048]{1,0:T(8,128)(2,1)S(1)}, bf16[64,2048]{1,0:T(8,128)(2,1)S(1)}, f32[8,2048]{1,0:T(8,128)S(1)}, bf16[4,256,1024]{2,1,0:T(8,128)(2,1)S(1)}, bf16[4,256,1024]{2,1,0:T(8,128)(2,1)S(1)}) custom-call(bf16[256,2048]{1,0:T(8,128)(2,1)S(1)} %convolution_convert_fusion.1.refs_0_, f32[64,2048]{1,0:T(8,128)S(1)} %get-tuple-element.83.refs_1_, ...), custom_call_target="tpu_custom_call" | custom-call | tf_op jit(solution)/shard_map/mlp_out/pallas_call | solution.py:197
  123.6 8.7 %multiply_convert_fusion = (bf16[256,2048]{1,0:T(8,128)(2,1)}, bf16[256,2048]{1,0:T(8,128)(2,1)S(1)}) fusion(f32[256,2048]{1,0:T(8,128)} %copy-done.76, f32[256,2048]{1,0:T(8,128)} %get-tuple-element.137, bf16[256,2048]{1,0:T(8,128)(2,1)} %copy-done.34, bf16[2048,2048]{1,0:T(8,128)(2,1)} %param.29), kind=kOutput, calls=%fused_computation.8 | convolution fusion | flops 2154299392 | bytes 15728640 | tf_op jit(solution)/shard_map/dot_general | solution.py:878
  132.3 7.1 %fusion.10 = f32[256,2048]{1,0:T(8,128)} fusion(bf16[256,2048]{1,0:T(8,128)(2,1)S(1)} %get-tuple-element.128.refs_6_, bf16[2048,2048]{1,0:T(8,128)(2,1)} %param.27), kind=kOutput, calls=%fused_computation.40 | convolution fusion | flops 2147483648 | bytes 11534336 | tf_op jit(solution)/shard_map/dot_general | solution.py:878
  140.5 6.8 %fusion.refs_0_ = bf16[256,2048]{1,0:T(8,128)(2,1)S(1)} fusion(f32[256,2048]{1,0:T(8,128)} %fusion.10, bf16[256,2048]{1,0:T(8,128)(2,1)} %get-tuple-element.127.refs_7_, bf16[2048,2048]{1,0:T(8,128)(2,1)} %param.28), kind=kOutput, calls=%fused_computation.3 | convolution fusion | flops 2148532224 | bytes 12582912 | tf_op jit(solution)/shard_map/dot_general | solution.py:878
  147.4 26.3 %mlp_back.1 = (bf16[256,2048]{1,0:T(8,128)(2,1)S(1)}, f32[64,2048]{1,0:T(8,128)S(1)}, f32[8,2048]{1,0:T(8,128)S(1)}, bf16[4,256,1024]{2,1,0:T(8,128)(2,1)S(1)}, ...) custom-call(bf16[256,2048]{1,0:T(8,128)(2,1)S(1)} %fusion.refs_0_, f32[64,2048]{1,0:T(8,128)S(1)} %copy-done.45, ...), custom_call_target="tpu_custom_call" | custom-call | tf_op jit(solution)/shard_map/mlp_back/pallas_call | solution.py:197
  174.6 6.2 %mlp_in.1.refs_11_ = bf16[4,2,4,64,1024]{4,3,2,1,0:T(8,128)(2,1)S(1)} custom-call(s32[1]{0:T(128)} %bitcast.7.core_ref, bf16[4,256,1024]{2,1,0:T(8,128)(2,1)S(1)} %copy-done.17, bf16[4,256,1024]{2,1,0:T(8,128)(2,1)S(1)} %get-tuple-element.97.other_half, bf16[4,256,512]{2,1,0:T(8,128)(2,1)S(1)} %get-tuple-element.98.refs_0_, ...), custom_call_target="tpu_custom_call" | custom-call | flops 4294967296 | bytes 10485760 | tf_op jit(solution)/shard_map/mlp_in/pallas_call | solution.py:843
  180.8 2.0 copy-done.5
  182.9 80.2 %attend_back.1 = (bf16[256,512]{1,0:T(8,128)(2,1)S(1)}, bf16[256,512]{1,0:T(8,128)(2,1)S(1)}, bf16[256,512]{1,0:T(8,128)(2,1)S(1)}, f32[1,512]{1,0:T(1,128)S(1)}...) custom-call(bf16[256,512]{1,0:T(8,128)(2,1)S(1)} %convolution_conver, ...), custom_call_target="tpu_custom_call" | custom-call | tf_op jit(solution)/shard_map/attend_back/pallas_call | solution.py:197
  270.2 2.5 fusion.11
  276.8 4.4 %reduce_sum.81.refs_6_ = bf16[2,4,64,1024]{3,2,1,0:T(8,128)(2,1)} reduce(bf16[4,2,4,64,1024]{4,3,2,1,0:T(8,128)(2,1)} %get-tuple-element.105, bf16[]{:T(256)} %constant.75.clone.1), dimensions={0}, to_apply=%region_0.0 | reduce | flops 1572864 | bytes 5242882 | tf_op jit(solution)/shard_map/reduce_sum | solution.py:859
  288.0 37.8 %input_grad.1 = (bf16[256,2048]{1,0:T(8,128)(2,1)S(1)}, bf16[4,256,128]{2,1,0:T(8,128)(2,1)S(1)}, bf16[4,256,128]{2,1,0:T(8,128)(2,1)S(1)}, bf16[4,256,128]{2,1,...) custom-call(bf16[256,2048]{1,0:T(8,128)(2,1)S(1)} %fusion.1.refs_0_,, ...), custom_call_target="tpu_custom_call" | custom-call | tf_op jit(solution)/shard_map/input_grad/pallas_call | solution.py:197
  330.7 3.7 mlp_down.1.refs_1_
  340.0 4.7 %qkv.1.refs_0_ = bf16[4,2,4,64,384]{4,3,2,1,0:T(8,128)(2,1)S(1)} custom-call(s32[1]{0:T(128)} %bitcast.7.core_ref, bf16[4,256,1024]{2,1,0:T(8,128)(2,1)S(1)} %copy-done.2, bf16[4,256,1024]{2,1,0:T(8,128)(2,1)S(1)} %copy-done.12, bf16[4,256,128]{2,1,0:T(8,128)(2,1)S(1)} %copy-done.52, bf16[4,256,128]{2,1,0:T(8,128)(2,1)S(1)} %copy-done.54, ...), custom_call_target="tpu_custom_call" | custom-call | flops 1610612736 | bytes 6553600 | tf_op jit(solution)/shard_map/qkv/pallas_call | solution.py:843
  344.7 34.0 %scatter.13 = (bf16[4,2,4,64,384]{4,3,2,1,0:T(8,128)(2,1)S(1)}, bf16[4,2,4,64,512]{4,3,2,1,0:T(8,128)(2,1)S(1)}, f32[32,8,128]{2,1,0:T(8,128)S(1)}) custom-call(bf16[4,2,4,64,384]{4,3,2,1,0:T(8,128)(2,1)S(1)} %qkv.1.refs_0_, bf16[4,2,4,64,512]{4,3,2,1,0:T(8,128)(2,1)S(1)} %copy-done.14, f32[32,8,128]{2,1,0:T(8,128)S(1)} %scatter.12.refs_2_), custom_call_target="tpu_custom_call" | custom-call | tf_op jit(solution)/shard_map/scatter/pallas_call | solution.py:197
  381.2 2.0 reduce_sum.83.refs_1_
  383.2 1.7 reduce_sum.82.refs_0_
  384.9 14.1 %place.1 = (bf16[2,4,64,384]{3,2,1,0:T(8,128)(2,1)S(1)}, bf16[2,4,64,512]{3,2,1,0:T(8,128)(2,1)S(1)}) custom-call(bf16[2,4,64,384]{3,2,1,0:T(8,128)(2,1)S(1)} %reduce_sum.82.refs_0_, bf16[2,4,64,512]{3,2,1,0:T(8,128)(2,1)S(1)} %reduce_sum.83.refs_1_), custom_call_target="tpu_custom_call" | custom-call | tf_op jit(solution)/shard_map/place/pallas_call | solution.py:197
  406.1 2.3 copy.66
  (199 shorter events, 51.1 us)
Async XLA Ops:
  7.2 39.3 %copy-start = (bf16[512,2048]{1,0:T(8,128)(2,1)S(1)}, bf16[512,2048]{1,0:T(8,128)(2,1)}, u32[]{:S(2)}) copy-start(bf16[512,2048]{1,0:T(8,128)(2,1)} %param.23) | copy-start | bytes 6291460
  7.2 398.9 %all-gather.2.cloned.1.call-start = ((), (), s32[]{:S(2)}) async-start(), calls=%async_computation | async-start | bytes 1310720 | tf_op jit(solution)/shard_map/all_gather | solution.py:901
  12.0 34.5 %copy-start.20 = (f32[256,512]{1,0:T(8,128)}, f32[256,512]{1,0:T(8,128)S(1)}, u32[]{:S(2)}) copy-start(f32[256,512]{1,0:T(8,128)S(1)} %fusion.7.refs_0_.refs_5_) | copy-start | bytes 1572868
  12.0 66.5 %copy-start.75 = (bf16[2048,2048]{1,0:T(8,128)(2,1)S(1)}, bf16[2048,2048]{1,0:T(8,128)(2,1)}, u32[]{:S(2)}) copy-start(bf16[2048,2048]{1,0:T(8,128)(2,1)} %param.27) | copy-start | bytes 25165828
  12.8 34.5 %copy-start.59 = (f32[2048]{0:T(1024)S(1)}, f32[2048]{0:T(1024)}, u32[]{:S(2)}) copy-start(f32[2048]{0:T(1024)} %param.26) | copy-start | bytes 24580
  46.4 30.2 %copy-start.4 = (bf16[4,256,2048]{2,1,0:T(8,128)(2,1)}, bf16[4,256,2048]{2,1,0:T(8,128)(2,1)S(1)}, u32[]{:S(2)}) copy-start(bf16[4,256,2048]{2,1,0:T(8,128)(2,1)S(1)} %get-tuple-element.94.refs_4_) | copy-start | bytes 12582916
  46.5 30.2 %copy-start.46 = (bf16[2048,128]{1,0:T(8,128)(2,1)}, bf16[2048,128]{1,0:T(8,128)(2,1)S(1)}, u32[]{:S(2)}) copy-start(bf16[2048,128]{1,0:T(8,128)(2,1)S(1)} %get-tuple-element.92.refs_2_) | copy-start | bytes 1572868
  46.5 30.2 %copy-start.48 = (bf16[2048,128]{1,0:T(8,128)(2,1)}, bf16[2048,128]{1,0:T(8,128)(2,1)S(1)}, u32[]{:S(2)}) copy-start(bf16[2048,128]{1,0:T(8,128)(2,1)S(1)} %get-tuple-element.93.refs_3_) | copy-start | bytes 1572868
  78.5 12.8 %copy-start.1 = (bf16[4,256,1024]{2,1,0:T(8,128)(2,1)}, bf16[4,256,1024]{2,1,0:T(8,128)(2,1)S(1)}, u32[]{:S(2)}) copy-start(bf16[4,256,1024]{2,1,0:T(8,128)(2,1)S(1)} %get-tuple-element.84.refs_5_.own_half) | copy-start | bytes 6291460
  78.5 10.4 %slice-start = ((s8[8388608]{0:T(1024)(128)(4,1)}), s8[4194304]{0:T(1024)(128)(4,1)S(1)}, s32[]{:S(2)}) async-start(s8[8388608]{0:T(1024)(128)(4,1)} %bitcast.108), calls=%async_computation.1 | async-start | bytes 8388608
  80.8 8.1 %copy-start.76 = (f32[256,2048]{1,0:T(8,128)}, f32[256,2048]{1,0:T(8,128)S(1)}, u32[]{:S(2)}) copy-start(f32[256,2048]{1,0:T(8,128)S(1)} %fusion.9) | copy-start | bytes 6291460
  80.8 8.1 %slice-start.1 = ((s8[8388608]{0:T(1024)(128)(4,1)}), s8[4194304]{0:T(1024)(128)(4,1)S(1)}, s32[]{:S(2)}) async-start(s8[8388608]{0:T(1024)(128)(4,1)} %bitcast.108), calls=%async_computation.2 | async-start | bytes 8388608
  140.5 6.8 %copy-start.31 = (bf16[256,2048]{1,0:T(8,128)(2,1)S(1)}, bf16[256,2048]{1,0:T(8,128)(2,1)}, u32[]{:S(2)}) copy-start(bf16[256,2048]{1,0:T(8,128)(2,1)} %copy-done.30) | copy-start | bytes 3145732
  140.5 6.8 %copy-start.45 = (f32[64,2048]{1,0:T(8,128)S(1)}, f32[64,2048]{1,0:T(8,128)}, u32[]{:S(2)}) copy-start(f32[64,2048]{1,0:T(8,128)} %copy-done.44) | copy-start | bytes 1572868
  140.5 6.9 %copy-start.58 = (f32[8,2048]{1,0:T(8,128)S(1)}, f32[8,2048]{1,0:T(8,128)}, u32[]{:S(2)}) copy-start(f32[8,2048]{1,0:T(8,128)} %copy-done.57) | copy-start | bytes 196612
  174.6 8.3 %copy-start.19 = (f32[256,512]{1,0:T(8,128)S(1)}, f32[256,512]{1,0:T(8,128)}, u32[]{:S(2)}) copy-start(f32[256,512]{1,0:T(8,128)} %copy-done.18) | copy-start | bytes 1572868
  174.6 8.3 %copy-start.21 = (f32[256,512]{1,0:T(8,128)S(1)}, f32[256,512]{1,0:T(8,128)}, u32[]{:S(2)}) copy-start(f32[256,512]{1,0:T(8,128)} %copy-done.20) | copy-start | bytes 1572868
  174.6 8.3 %copy-start.33 = (bf16[256,2048]{1,0:T(8,128)(2,1)S(1)}, bf16[256,2048]{1,0:T(8,128)(2,1)}, u32[]{:S(2)}) copy-start(bf16[256,2048]{1,0:T(8,128)(2,1)} %copy-done.32) | copy-start | bytes 3145732
  174.6 8.3 %copy-start.35 = (bf16[256,2048]{1,0:T(8,128)(2,1)S(1)}, bf16[256,2048]{1,0:T(8,128)(2,1)}, u32[]{:S(2)}) copy-start(bf16[256,2048]{1,0:T(8,128)(2,1)} %copy-done.34) | copy-start | bytes 3145732
  174.6 8.3 %copy-start.47 = (bf16[2048,128]{1,0:T(8,128)(2,1)S(1)}, bf16[2048,128]{1,0:T(8,128)(2,1)}, u32[]{:S(2)}) copy-start(bf16[2048,128]{1,0:T(8,128)(2,1)} %copy-done.46) | copy-start | bytes 1572868
  174.6 8.3 %copy-start.49 = (bf16[2048,128]{1,0:T(8,128)(2,1)S(1)}, bf16[2048,128]{1,0:T(8,128)(2,1)}, u32[]{:S(2)}) copy-start(bf16[2048,128]{1,0:T(8,128)(2,1)} %copy-done.48) | copy-start | bytes 1572868
  267.1 7.2 %copy-start.23 = (bf16[256,512]{1,0:T(8,128)(2,1)}, bf16[256,512]{1,0:T(8,128)(2,1)S(1)}, u32[]{:S(2)}) copy-start(bf16[256,512]{1,0:T(8,128)(2,1)S(1)} %get-tuple-element.101.refs_3_) | copy-start | bytes 786436
  288.0 42.7 %copy-start.10 = (bf16[4,256,1024]{2,1,0:T(8,128)(2,1)S(1)}, bf16[4,256,1024]{2,1,0:T(8,128)(2,1)}, u32[]{:S(2)}) copy-start(bf16[4,256,1024]{2,1,0:T(8,128)(2,1)} %copy-done.8) | copy-start | bytes 6291460
  288.0 42.7 %copy-start.67 = (bf16[4,256,512]{2,1,0:T(8,128)(2,1)S(1)}, bf16[4,256,512]{2,1,0:T(8,128)(2,1)}, u32[]{:S(2)}) copy-start(bf16[4,256,512]{2,1,0:T(8,128)(2,1)} %copy-done.66) | copy-start | bytes 3145732
  (56 other events, 114.0 us)
Sparse Core Ops, SparseCore 0:
  123.7 17.9 all-gather.1
